TPU v7x, 32 devices: a whole 2x2x4 slice. The times are simulated.
32 devices in a mesh: dp: 4 (over y, core), ctx: 8 (over z, x).
Axes of the slice: x: 2, y: 2, z: 4, core: 2. Of those that a mesh axis runs over, the one named last changes fastest.
Arguments:
- out_gate: bfloat16 [4, 2048, 512], P('dp', 'ctx'), may hold values from -6 to 6
- key_gate: bfloat16 [4, 2048, 512], P('dp', 'ctx'), may hold values from -6 to 6
- value_input: bfloat16 [4, 2048, 512], P('dp', 'ctx'), may hold values from -6 to 6
- filter_taps: bfloat16 [2048, 512], P('ctx'), may hold values from -2 to 2
- cotangent: bfloat16 [4, 2048, 512], P('dp', 'ctx'), may hold values from -6 to 6
- block_live: int32 [4, 32], P('dp', 'ctx'), may hold values 0 or 1
Outputs:
- grad_out_gate: bfloat16 [4, 2048, 512], P('dp', 'ctx')
- grad_key_gate: bfloat16 [4, 2048, 512], P('dp', 'ctx')
- grad_value: bfloat16 [4, 2048, 512], P('dp', 'ctx')
- grad_taps: bfloat16 [2048, 512], P('ctx')
Inputs may be any that keep to these rules, and one draw needn't show every extreme that they name: `block_live`: 1 where a block of 64 tokens holds sequence data, 0 where it is padding.
All inputs are finite; a program needn't handle non-finite values.
Results may differ from a plain program's by a relative error of at most 0.027.
Values may be sent and summed in bfloat16 or wider, within the bound.
No kernel may reach another device: no remote copies, remote signals or barrier semaphores. Data moves between devices by JAX's collectives and lax.ppermute only.
A program may use at most 64 MiB of HBM per device.

v0:
```python
import math

import jax
import jax.numpy as jnp
from jax import lax
from jax.sharding import PartitionSpec as P

QLEN = 64
PROWS = 4


TWO_PI = 2.0 * math.pi


def angle_table(row_count, col_count, row_start, col_start, period_len, direction):
    row_ids = jnp.arange(row_count, dtype=jnp.int32)[:, None] + row_start
    col_ids = jnp.arange(col_count, dtype=jnp.int32)[None, :] + col_start
    phases = (row_ids * col_ids % period_len).astype(jnp.float32)
    return direction * TWO_PI * phases / period_len


def factor_tables(angles):
    return (jnp.cos(angles).astype(jnp.bfloat16), jnp.sin(angles).astype(jnp.bfloat16))


def rotate_pair(real_part, imag_part, angles):
    turn_cos = jnp.cos(angles)[None, :, :, None]
    turn_sin = jnp.sin(angles)[None, :, :, None]
    return (
        real_part * turn_cos - imag_part * turn_sin,
        real_part * turn_sin + imag_part * turn_cos,
    )


def forward_transform(signals):
    ctx_count = lax.axis_size("ctx")
    ctx_place = lax.axis_index("ctx")
    full_rows = 2 * signals.shape[1] * ctx_count
    col_count = signals.shape[2]
    col_share = col_count // ctx_count
    total_len = full_rows * col_count
    cos_rows, sin_rows = factor_tables(
        angle_table(full_rows, full_rows // 2, 0, 0, full_rows, -1.0)
    )
    twist_angles = angle_table(full_rows, col_share, 0, ctx_place * col_share, total_len, -1.0)
    cos_cols, sin_cols = factor_tables(angle_table(col_count, col_count, 0, 0, col_count, -1.0))
    spread = lax.all_to_all(signals, "ctx", split_axis=2, concat_axis=1, tiled=True)
    real_part = jnp.einsum("kp,spac->skac", cos_rows, spread, preferred_element_type=jnp.float32)
    imag_part = jnp.einsum("kp,spac->skac", sin_rows, spread, preferred_element_type=jnp.float32)
    real_part, imag_part = rotate_pair(real_part, imag_part, twist_angles)
    packed = jnp.stack([real_part, imag_part]).astype(jnp.bfloat16)
    regrouped = lax.all_to_all(packed, "ctx", split_axis=2, concat_axis=3, tiled=True)
    real_in = regrouped[0]
    imag_in = regrouped[1]
    real_out = jnp.einsum(
        "saqc,qk->sakc", real_in, cos_cols, preferred_element_type=jnp.float32
    ) - jnp.einsum("saqc,qk->sakc", imag_in, sin_cols, preferred_element_type=jnp.float32)
    imag_out = jnp.einsum(
        "saqc,qk->sakc", real_in, sin_cols, preferred_element_type=jnp.float32
    ) + jnp.einsum("saqc,qk->sakc", imag_in, cos_cols, preferred_element_type=jnp.float32)
    return jnp.stack([real_out, imag_out]).astype(jnp.bfloat16)


def inverse_transform(spectra):
    ctx_count = lax.axis_size("ctx")
    ctx_place = lax.axis_index("ctx")
    row_share = spectra.shape[2]
    col_count = spectra.shape[3]
    full_rows = row_share * ctx_count
    total_len = full_rows * col_count
    cos_cols, sin_cols = factor_tables(angle_table(col_count, col_count, 0, 0, col_count, 1.0))
    twist_angles = angle_table(row_share, col_count, ctx_place * row_share, 0, total_len, 1.0)
    cos_back, sin_back = factor_tables(angle_table(full_rows // 2, full_rows, 0, 0, full_rows, 1.0))
    real_in = spectra[0]
    imag_in = spectra[1]
    real_part = jnp.einsum(
        "sakc,kq->saqc", real_in, cos_cols, preferred_element_type=jnp.float32
    ) - jnp.einsum("sakc,kq->saqc", imag_in, sin_cols, preferred_element_type=jnp.float32)
    imag_part = jnp.einsum(
        "sakc,kq->saqc", real_in, sin_cols, preferred_element_type=jnp.float32
    ) + jnp.einsum("sakc,kq->saqc", imag_in, cos_cols, preferred_element_type=jnp.float32)
    real_part, imag_part = rotate_pair(real_part, imag_part, twist_angles)
    twisted = jnp.stack([real_part, imag_part]).astype(jnp.bfloat16)
    gathered = lax.all_to_all(twisted, "ctx", split_axis=3, concat_axis=2, tiled=True)
    signal = jnp.einsum(
        "pk,skac->spac", cos_back, gathered[0], preferred_element_type=jnp.float32
    ) - jnp.einsum("pk,skac->spac", sin_back, gathered[1], preferred_element_type=jnp.float32)
    spread = (signal * (1.0 / total_len)).astype(jnp.bfloat16)
    return lax.all_to_all(spread, "ctx", split_axis=1, concat_axis=2, tiled=True)


def spectrum_product(left_spec, right_spec, conjugate):
    left_real = left_spec[0].astype(jnp.float32)
    left_imag = left_spec[1].astype(jnp.float32)
    right_real = right_spec[0].astype(jnp.float32)
    right_imag = right_spec[1].astype(jnp.float32)
    if conjugate:
        real_out = left_real * right_real + left_imag * right_imag
        imag_out = left_imag * right_real - left_real * right_imag
    else:
        real_out = left_real * right_real - left_imag * right_imag
        imag_out = left_real * right_imag + left_imag * right_real
    return jnp.stack([real_out, imag_out]).astype(jnp.bfloat16)


def local(out_gate, key_gate, value_input, filter_taps, cotangent, block_live):
    tok_count = key_gate.shape[1]
    chan_count = key_gate.shape[2]
    block_count = block_live.shape[1]
    grid_shape = (PROWS, QLEN, chan_count)
    live_rows = block_live[0].astype(jnp.float32)[:, None, None]

    def masked(values):
        return (
            values.reshape(block_count, tok_count // block_count, chan_count) * live_rows
        ).reshape(tok_count, chan_count)

    key_wide = key_gate[0].astype(jnp.float32)
    value_wide = value_input[0].astype(jnp.float32)
    cot_wide = cotangent[0].astype(jnp.float32)
    gated_input = masked(key_wide * value_wide).astype(jnp.bfloat16).reshape(grid_shape)
    back_signal = (
        (cot_wide * out_gate[0].astype(jnp.float32)).astype(jnp.bfloat16).reshape(grid_shape)
    )
    taps_grid = filter_taps.reshape(grid_shape)
    filter_spec = None
    extra_signals = [taps_grid]
    first_spectra = forward_transform(jnp.stack([gated_input] + extra_signals))
    filter_spec = first_spectra[:, 1]
    forward_spec = first_spectra[:, 0]
    conv_out = inverse_transform(spectrum_product(forward_spec, filter_spec, False)[:, None])[0]
    backward_spec = forward_transform(back_signal[None])[:, 0]
    restored = inverse_transform(
        jnp.stack(
            [
                spectrum_product(backward_spec, filter_spec, True),
                spectrum_product(backward_spec, forward_spec, True),
            ],
            axis=1,
        )
    )
    grad_conv = restored[0]
    taps_seq = restored[1]
    conv_flat = conv_out.reshape(tok_count, chan_count).astype(jnp.float32)
    grad_gate = (cot_wide * conv_flat).astype(jnp.bfloat16)
    grad_flat = grad_conv.reshape(tok_count, chan_count).astype(jnp.float32)
    grad_key = masked(grad_flat * value_wide).astype(jnp.bfloat16)
    grad_value = masked(grad_flat * key_wide).astype(jnp.bfloat16)
    scale_factor = 1.0 / math.sqrt(lax.axis_size("dp") * tok_count * lax.axis_size("ctx"))
    taps_sum = lax.psum(
        taps_seq.reshape(tok_count, chan_count).astype(jnp.float32).astype(jnp.bfloat16), "dp"
    ).astype(jnp.float32)
    grad_taps = (taps_sum * scale_factor).astype(jnp.bfloat16)
    return (grad_gate[None], grad_key[None], grad_value[None], grad_taps)


def solution(mesh):
    return jax.shard_map(
        local,
        mesh=mesh,
        in_specs=(
            P("dp", "ctx", None),
            P("dp", "ctx", None),
            P("dp", "ctx", None),
            P("ctx", None),
            P("dp", "ctx", None),
            P("dp", "ctx"),
        ),
        out_specs=(
            P("dp", "ctx", None),
            P("dp", "ctx", None),
            P("dp", "ctx", None),
            P("ctx", None),
        ),
        check_vma=False,
    )
```

profile of v0, /device:TPU:0, one launch (start us, length us, event | category | flops | bytes accessed | tf_op | source)
XLA Modules:
  0.0 287.2 jit_solution(15217208088847125802)
XLA Ops:
  7.2 1.1 fusion.48
  8.3 0.9 copy.60
  9.2 7.3 %all-to-all-start.4 = ((bf16[1,4,64,512]{3,1,0,2:T(4,128)(2,1)}), bf16[1,4,64,512]{3,1,0,2:T(4,128)(2,1)S(1)}, u32[]{:S(2)}, u32[]{:S(2)}) async-start(bf16[1,4,64,512]{3,1,0,2:T(4,128)(2,1)} %copy.60), calls=%async_computation.4 | async-start | bytes 524288 | tf_op jit(solution)/shard_map/all_to_all | solution.py:47
  16.5 1.1 convert_multiply_fusion.14
  17.8 1.2 copy.51
  19.0 6.4 %all-to-all-done.4 = bf16[1,4,64,512]{3,1,0,2:T(4,128)(2,1)S(1)} async-done(((bf16[1,4,64,512]{3,1,0,2:T(4,128)(2,1)}), bf16[1,4,64,512]{3,1,0,2:T(4,128)(2,1)S(1)}, u32[]{:S(2)}, u32[]{:S(2)}) %all-to-all-start.4) | async-done | bytes 262176 | tf_op jit(solution)/shard_map/all_to_all | solution.py:47
  25.4 3.6 %all-to-all-start = ((bf16[2,4,64,512]{3,1,0,2:T(4,128)(2,1)}), bf16[2,4,64,512]{3,1,0,2:T(4,128)(2,1)S(1)}, u32[]{:S(2)}, u32[]{:S(2)}) async-start(bf16[2,4,64,512]{3,1,0,2:T(4,128)(2,1)} %copy.51), calls=%async_computation | async-start | bytes 1048576 | tf_op jit(solution)/shard_map/all_to_all | solution.py:47
  29.9 0.6 fusion.55
  30.6 1.6 copy.63
  32.2 11.0 %all-to-all-done = bf16[2,4,64,512]{3,1,0,2:T(4,128)(2,1)S(1)} async-done(((bf16[2,4,64,512]{3,1,0,2:T(4,128)(2,1)}), bf16[2,4,64,512]{3,1,0,2:T(4,128)(2,1)S(1)}, u32[]{:S(2)}, u32[]{:S(2)}) %all-to-all-start) | async-done | bytes 524320 | tf_op jit(solution)/shard_map/all_to_all | solution.py:47
  43.2 3.6 %all-to-all-start.5 = ((bf16[2,1,64,8,512]{4,3,1,0,2:T(8,128)(2,1)}), bf16[2,1,64,8,512]{4,3,1,0,2:T(8,128)(2,1)S(1)}, u32[]{:S(2)}, u32[]{:S(2)}) async-start(bf16[2,1,64,8,512]{4,3,1,0,2:T(8,128)(2,1)} %copy.63), calls=%async_computation.5 | async-start | bytes 2097152 | tf_op jit(solution)/shard_map/all_to_all | solution.py:52
  47.5 0.6 fusion.99
  48.1 1.0 fusion.39
  49.3 2.5 copy.54
  51.9 20.7 %all-to-all-done.5 = bf16[2,1,64,8,512]{4,3,1,0,2:T(8,128)(2,1)S(1)} async-done(((bf16[2,1,64,8,512]{4,3,1,0,2:T(8,128)(2,1)}), bf16[2,1,64,8,512]{4,3,1,0,2:T(8,128)(2,1)S(1)}, u32[]{:S(2)}, u32[]{:S(2)}) %all-to-all-start.5) | async-done | bytes 1048608 | tf_op jit(solution)/shard_map/all_to_all | solution.py:52
  72.5 1.0 copy-done
  73.5 3.8 %all-to-all-start.1 = ((bf16[2,2,64,8,512]{4,3,1,0,2:T(8,128)(2,1)}), bf16[2,2,64,8,512]{4,3,1,0,2:T(8,128)(2,1)S(1)}, u32[]{:S(2)}, u32[]{:S(2)}) async-start(bf16[2,2,64,8,512]{4,3,1,0,2:T(8,128)(2,1)} %copy.54), calls=%async_computation.1 | async-start | bytes 4194304 | tf_op jit(solution)/shard_map/all_to_all | solution.py:52
  77.4 1.3 copy.86
  79.2 1.4 fusion.18
  80.6 1.4 fusion.61
  82.0 43.6 %all-to-all-done.1 = bf16[2,2,64,8,512]{4,3,1,0,2:T(8,128)(2,1)S(1)} async-done(((bf16[2,2,64,8,512]{4,3,1,0,2:T(8,128)(2,1)}), bf16[2,2,64,8,512]{4,3,1,0,2:T(8,128)(2,1)S(1)}, u32[]{:S(2)}, u32[]{:S(2)}) %all-to-all-start.1) | async-done | bytes 2097184 | tf_op jit(solution)/shard_map/all_to_all | solution.py:52
  125.9 0.5 fusion.43
  126.9 0.5 fusion.9
  127.5 0.5 fusion.8
  128.0 0.7 copy-done.1
  129.0 2.1 fusion.33
  132.3 0.6 fusion.53
  133.0 1.6 copy.56
  134.6 3.6 %all-to-all-start.2 = ((bf16[2,1,8,64,512]{4,2,1,0,3:T(8,128)(2,1)}), bf16[2,1,8,64,512]{4,2,1,0,3:T(8,128)(2,1)S(1)}, u32[]{:S(2)}, u32[]{:S(2)}) async-start(bf16[2,1,8,64,512]{4,2,1,0,3:T(8,128)(2,1)} %copy.56), calls=%async_computation.2 | async-start | bytes 2097152 | tf_op jit(solution)/shard_map/all_to_all | solution.py:84
  138.4 0.5 fusion.45
  138.9 0.5 fusion.46
  139.4 0.5 convolution_add_fusion
  139.9 0.9 fusion.41
  141.1 2.5 copy.65
  143.6 20.5 %all-to-all-done.2 = bf16[2,1,8,64,512]{4,2,1,0,3:T(8,128)(2,1)S(1)} async-done(((bf16[2,1,8,64,512]{4,2,1,0,3:T(8,128)(2,1)}), bf16[2,1,8,64,512]{4,2,1,0,3:T(8,128)(2,1)S(1)}, u32[]{:S(2)}, u32[]{:S(2)}) %all-to-all-start.2) | async-done | bytes 1048608 | tf_op jit(solution)/shard_map/all_to_all | solution.py:84
  164.1 3.6 %all-to-all-start.6 = ((bf16[2,2,8,64,512]{4,2,1,0,3:T(8,128)(2,1)}), bf16[2,2,8,64,512]{4,2,1,0,3:T(8,128)(2,1)S(1)}, u32[]{:S(2)}, u32[]{:S(2)}) async-start(bf16[2,2,8,64,512]{4,2,1,0,3:T(8,128)(2,1)} %copy.65), calls=%async_computation.6 | async-start | bytes 4194304 | tf_op jit(solution)/shard_map/all_to_all | solution.py:84
  168.4 0.9 copy.58
  169.3 46.9 %all-to-all-done.6 = bf16[2,2,8,64,512]{4,2,1,0,3:T(8,128)(2,1)S(1)} async-done(((bf16[2,2,8,64,512]{4,2,1,0,3:T(8,128)(2,1)}), bf16[2,2,8,64,512]{4,2,1,0,3:T(8,128)(2,1)S(1)}, u32[]{:S(2)}, u32[]{:S(2)}) %all-to-all-start.6) | async-done | bytes 2097184 | tf_op jit(solution)/shard_map/all_to_all | solution.py:84
  216.1 3.6 %all-to-all-start.3 = ((bf16[1,32,8,512]{3,2,0,1:T(8,128)(2,1)}), bf16[1,32,8,512]{3,2,0,1:T(8,128)(2,1)S(1)}, u32[]{:S(2)}, u32[]{:S(2)}) async-start(bf16[1,32,8,512]{3,2,0,1:T(8,128)(2,1)} %copy.58), calls=%async_computation.3 | async-start | bytes 524288 | tf_op jit(solution)/shard_map/all_to_all | solution.py:89
  220.8 1.1 copy.67
  221.9 7.0 %all-to-all-done.3 = bf16[1,32,8,512]{3,2,0,1:T(8,128)(2,1)S(1)} async-done(((bf16[1,32,8,512]{3,2,0,1:T(8,128)(2,1)}), bf16[1,32,8,512]{3,2,0,1:T(8,128)(2,1)S(1)}, u32[]{:S(2)}, u32[]{:S(2)}) %all-to-all-start.3) | async-done | bytes 262176 | tf_op jit(solution)/shard_map/all_to_all | solution.py:89
  228.9 3.6 %all-to-all-start.7 = ((bf16[2,32,8,512]{3,2,0,1:T(8,128)(2,1)}), bf16[2,32,8,512]{3,2,0,1:T(8,128)(2,1)S(1)}, u32[]{:S(2)}, u32[]{:S(2)}) async-start(bf16[2,32,8,512]{3,2,0,1:T(8,128)(2,1)} %copy.67), calls=%async_computation.7 | async-start | bytes 1048576 | tf_op jit(solution)/shard_map/all_to_all | solution.py:89
  232.7 0.8 fusion.47
  233.5 13.1 %all-to-all-done.7 = bf16[2,32,8,512]{3,2,0,1:T(8,128)(2,1)S(1)} async-done(((bf16[2,32,8,512]{3,2,0,1:T(8,128)(2,1)}), bf16[2,32,8,512]{3,2,0,1:T(8,128)(2,1)S(1)}, u32[]{:S(2)}, u32[]{:S(2)}) %all-to-all-start.7) | async-done | bytes 524320 | tf_op jit(solution)/shard_map/all_to_all | solution.py:89
  246.7 0.7 fusion.219
  247.5 1.0 fusion.52
  248.4 30.2 %all-reduce.2.cloned.1.call-done = bf16[256,512]{1,0:T(8,128)(2,1)} async-done(((bf16[256,512]{1,0:T(8,128)(2,1)}), bf16[256,512]{1,0:T(8,128)(2,1)}) %all-reduce.2.cloned.1.call-update) | async-done | bytes 262160 | tf_op jit(solution)/shard_map/psum | solution.py:150
  278.7 1.7 multiply_convert_fusion
  (54 shorter events, 7.3 us)
Async XLA Ops:
  7.2 10.4 %copy-start.9 = (s32[1,4]{1,0:T(1,128)S(1)}, s32[1,4]{1,0:T(1,128)}, u32[]{:S(2)}) copy-start(s32[1,4]{1,0:T(1,128)} %param.11) | copy-start | bytes 52
  7.2 10.5 %copy-start.8 = (bf16[256,512]{1,0:T(8,128)(2,1)S(1)}, bf16[256,512]{1,0:T(8,128)(2,1)}, u32[]{:S(2)}) copy-start(bf16[256,512]{1,0:T(8,128)(2,1)} %param.9) | copy-start | bytes 786436
  9.2 16.2 %all-to-all-start.4 = ((bf16[1,4,64,512]{3,1,0,2:T(4,128)(2,1)}), bf16[1,4,64,512]{3,1,0,2:T(4,128)(2,1)S(1)}, u32[]{:S(2)}, u32[]{:S(2)}) async-start(bf16[1,4,64,512]{3,1,0,2:T(4,128)(2,1)} %copy.60), calls=%async_computation.4 | async-start | bytes 524288 | tf_op jit(solution)/shard_map/all_to_all | solution.py:47
  25.4 17.8 %all-to-all-start = ((bf16[2,4,64,512]{3,1,0,2:T(4,128)(2,1)}), bf16[2,4,64,512]{3,1,0,2:T(4,128)(2,1)S(1)}, u32[]{:S(2)}, u32[]{:S(2)}) async-start(bf16[2,4,64,512]{3,1,0,2:T(4,128)(2,1)} %copy.51), calls=%async_computation | async-start | bytes 1048576 | tf_op jit(solution)/shard_map/all_to_all | solution.py:47
  43.2 29.4 %all-to-all-start.5 = ((bf16[2,1,64,8,512]{4,3,1,0,2:T(8,128)(2,1)}), bf16[2,1,64,8,512]{4,3,1,0,2:T(8,128)(2,1)S(1)}, u32[]{:S(2)}, u32[]{:S(2)}) async-start(bf16[2,1,64,8,512]{4,3,1,0,2:T(8,128)(2,1)} %copy.63), calls=%async_computation.5 | async-start | bytes 2097152 | tf_op jit(solution)/shard_map/all_to_all | solution.py:52
  72.5 1.0 copy-start
  73.5 52.1 %all-to-all-start.1 = ((bf16[2,2,64,8,512]{4,3,1,0,2:T(8,128)(2,1)}), bf16[2,2,64,8,512]{4,3,1,0,2:T(8,128)(2,1)S(1)}, u32[]{:S(2)}, u32[]{:S(2)}) async-start(bf16[2,2,64,8,512]{4,3,1,0,2:T(8,128)(2,1)} %copy.54), calls=%async_computation.1 | async-start | bytes 4194304 | tf_op jit(solution)/shard_map/all_to_all | solution.py:52
  127.5 1.2 copy-start.1
  127.5 1.5 copy-start.2
  133.0 5.2 %copy-start.6 = (bf16[1,1,8,64,512]{4,3,2,1,0:T(8,128)(2,1)S(1)}, bf16[1,1,8,64,512]{4,3,2,1,0:T(8,128)(2,1)}, u32[]{:S(2)}) copy-start(bf16[1,1,8,64,512]{4,3,2,1,0:T(8,128)(2,1)} %get-tuple-element.10) | copy-start | bytes 1572868
  133.0 5.2 %copy-start.7 = (bf16[1,1,8,64,512]{4,3,2,1,0:T(8,128)(2,1)S(1)}, bf16[1,1,8,64,512]{4,3,2,1,0:T(8,128)(2,1)}, u32[]{:S(2)}) copy-start(bf16[1,1,8,64,512]{4,3,2,1,0:T(8,128)(2,1)} %get-tuple-element.11) | copy-start | bytes 1572868
  134.6 29.5 %all-to-all-start.2 = ((bf16[2,1,8,64,512]{4,2,1,0,3:T(8,128)(2,1)}), bf16[2,1,8,64,512]{4,2,1,0,3:T(8,128)(2,1)S(1)}, u32[]{:S(2)}, u32[]{:S(2)}) async-start(bf16[2,1,8,64,512]{4,2,1,0,3:T(8,128)(2,1)} %copy.56), calls=%async_computation.2 | async-start | bytes 2097152 | tf_op jit(solution)/shard_map/all_to_all | solution.py:84
  164.1 52.1 %all-to-all-start.6 = ((bf16[2,2,8,64,512]{4,2,1,0,3:T(8,128)(2,1)}), bf16[2,2,8,64,512]{4,2,1,0,3:T(8,128)(2,1)S(1)}, u32[]{:S(2)}, u32[]{:S(2)}) async-start(bf16[2,2,8,64,512]{4,2,1,0,3:T(8,128)(2,1)} %copy.65), calls=%async_computation.6 | async-start | bytes 4194304 | tf_op jit(solution)/shard_map/all_to_all | solution.py:84
  216.1 12.7 %all-to-all-start.3 = ((bf16[1,32,8,512]{3,2,0,1:T(8,128)(2,1)}), bf16[1,32,8,512]{3,2,0,1:T(8,128)(2,1)S(1)}, u32[]{:S(2)}, u32[]{:S(2)}) async-start(bf16[1,32,8,512]{3,2,0,1:T(8,128)(2,1)} %copy.58), calls=%async_computation.3 | async-start | bytes 524288 | tf_op jit(solution)/shard_map/all_to_all | solution.py:89
  220.8 11.9 %copy-start.3 = (bf16[1,256,512]{2,1,0:T(8,128)(2,1)S(1)}, bf16[1,256,512]{2,1,0:T(8,128)(2,1)}, u32[]{:S(2)}) copy-start(bf16[1,256,512]{2,1,0:T(8,128)(2,1)} %param.10) | copy-start | bytes 786436
  228.9 17.8 %all-to-all-start.7 = ((bf16[2,32,8,512]{3,2,0,1:T(8,128)(2,1)}), bf16[2,32,8,512]{3,2,0,1:T(8,128)(2,1)S(1)}, u32[]{:S(2)}, u32[]{:S(2)}) async-start(bf16[2,32,8,512]{3,2,0,1:T(8,128)(2,1)} %copy.67), calls=%async_computation.7 | async-start | bytes 1048576 | tf_op jit(solution)/shard_map/all_to_all | solution.py:89
  232.5 46.2 %all-reduce.2.cloned.1.call-start = ((), (), s32[]{:S(2)}) async-start(), calls=%async_computation.8 | async-start | bytes 524288 | tf_op jit(solution)/shard_map/psum | solution.py:150
  232.7 14.8 %copy-start.4 = (bf16[1,256,512]{2,1,0:T(8,128)(2,1)S(1)}, bf16[1,256,512]{2,1,0:T(8,128)(2,1)}, u32[]{:S(2)}) copy-start(bf16[1,256,512]{2,1,0:T(8,128)(2,1)} %param.8) | copy-start | bytes 786436
  232.7 14.8 %copy-start.5 = (bf16[1,256,512]{2,1,0:T(8,128)(2,1)S(1)}, bf16[1,256,512]{2,1,0:T(8,128)(2,1)}, u32[]{:S(2)}) copy-start(bf16[1,256,512]{2,1,0:T(8,128)(2,1)} %param.7) | copy-start | bytes 786436
Sparse Core Ops, SparseCore 0:
  247.6 31.0 all-reduce.1
where the time goes:
time: 288 us; the launch traced here: 287 us
  waiting for transfers between devices  200 us (69%)
  starting transfers between devices  32.7 us (11%)
  local copies, waits for them, and re-layouts  18.2 us (6%)
  matrix products  15.6 us (5%)
  between operations  14.4 us (5%)
  other arithmetic  6.83 us (2%)
    all_to_all x2, waiting for transfers between devices, inverse_transform(): lax.all_to_all(twisted, 'ctx', split_axis=3, concat_axis=2, tiled=True)  67.4 us
    all_to_all x2, waiting for transfers between devices, forward_transform(): lax.all_to_all(packed, 'ctx', split_axis=2, concat_axis=3, tiled=True)  64.3 us
    psum x1, waiting for transfers between devices, local(): lax.psum(taps_seq.reshape(tok_count, chan_count).astype(jnp.float32).asty...  30.2 us
    all_to_all x2, waiting for transfers between devices, inverse_transform(): lax.all_to_all(spread, 'ctx', split_axis=1, concat_axis=2, tiled=True)  20.1 us
    all_to_all x2, waiting for transfers between devices, forward_transform(): lax.all_to_all(signals, 'ctx', split_axis=2, concat_axis=1, tiled=True)  17.4 us
    all_to_all x2, starting transfers between devices, forward_transform(): lax.all_to_all(signals, 'ctx', split_axis=2, concat_axis=1, tiled=True)  10.8 us
    all_to_all x2, starting transfers between devices, forward_transform(): lax.all_to_all(packed, 'ctx', split_axis=2, concat_axis=3, tiled=True)  7.42 us
    all_to_all x2, starting transfers between devices, inverse_transform(): lax.all_to_all(spread, 'ctx', split_axis=1, concat_axis=2, tiled=True)  7.22 us
  transfers between devices with their start and end apart: 9, of which 9 were waited for; matrix products, arithmetic and copies ran while one was open for 9% of the time, Pallas kernels for 0%

commit v1 on v0

v1 whole, which is shorter than its diff:
```python
import functools
import math

import jax
import jax.numpy as jnp
import ml_dtypes
import numpy as np
from jax import lax
from jax.experimental import pallas as pl
from jax.experimental.pallas import tpu as pltpu
from jax.sharding import PartitionSpec as P


SUB = 8
VMEM = 60 * 1024 * 1024
F32 = jnp.float32
BF16 = jnp.bfloat16


def transform_tables(prow, qlen):
    total = prow * qlen
    k1 = np.arange(prow)
    p = np.arange(prow)
    theta = 2.0 * np.pi * (((4 * k1[:, None] + 1) * p[None, :]) % (4 * prow)) / (4 * prow)
    eye = np.eye(SUB)
    first = np.stack([np.cos(theta), -np.sin(theta)], axis=1)
    first = np.einsum("krp,ab->krapb", first, eye).reshape(prow * 2 * SUB, prow * SUB)
    last = np.stack([np.cos(theta), -np.sin(theta)], axis=0) / total
    last = last.reshape(2, prow // 2, 2, prow)
    last = np.einsum("rmlp,ab->pamrlb", last, eye).reshape(prow * SUB, prow * 2 * SUB)
    q = np.arange(qlen)
    k2 = np.arange(qlen)
    phase = (4 * k1[:, None, None] + 1 + 4 * prow * k2[None, :, None]) * q[None, None, :]
    phi = 2.0 * np.pi * (phase % (4 * total)) / (4 * total)
    re, im = np.cos(phi), -np.sin(phi)
    mid = np.concatenate(
        [np.concatenate([re, -im], axis=2), np.concatenate([im, re], axis=2)], axis=1
    )
    back = np.swapaxes(mid, 1, 2)
    return [t.astype(ml_dtypes.bfloat16) for t in (first, mid, back, last)]


def dot(a, b):
    return jnp.dot(a, b, preferred_element_type=F32)


def prep_kernel(core, live, out_gate, key, value, cot, taps, out):
    groups = out.shape[0]
    share = out.shape[2] // 2
    blocks = live.shape[1]
    tok = key.shape[1]
    qlen = tok // blocks
    qblocks = qlen // SUB
    for p in range(0, blocks, 2):
        pair = []
        for e in (0, 1):
            rows = slice((p + e) * qlen, (p + e + 1) * qlen)
            alive = live[0, p + e].astype(F32)
            u = key[0, rows, :].astype(F32) * value[0, rows, :].astype(F32) * alive
            g = cot[0, rows, :].astype(F32) * out_gate[0, rows, :].astype(F32)
            pair.append((u, g))
        for j in range(groups):
            lanes = slice(j * share, (j + 1) * share)
            ends = [
                jnp.concatenate([u[:, lanes], g[:, lanes]], axis=1).reshape(qblocks, 1, SUB, 2 * share)
                for u, g in pair
            ]
            both = jnp.concatenate(ends, axis=1).reshape(qblocks, 2 * SUB, 2 * share).astype(BF16)
            for qb in range(qblocks):
                start = qb * blocks * SUB + p * SUB
                out[j, start : start + 2 * SUB, :] = both[qb]
    half = tok // 2
    mine = taps[pl.ds(pl.multiple_of(core[0] * half, half), half), :].astype(F32)
    for j in range(groups):
        lanes = slice(j * share, (j + 1) * share)
        both = jnp.concatenate([mine[:qlen, lanes], mine[qlen:, lanes]], axis=1)
        out[j, tok:, :] = both.astype(BF16)


def stage_one(first, load, rows, qblocks, dest):
    width = dest.shape[2]
    pairs = dest.shape[0]
    for qb in range(0, qblocks, 2):
        ends = [
            dot(first[...], load(qb + e)).reshape(pairs, SUB, width) for e in (0, 1)
        ]
        dest[:, qb * SUB : (qb + 2) * SUB, :] = jnp.concatenate(ends, axis=1).astype(BF16)


def store_pair(ends, m, qblocks, held):
    width = held.shape[2]
    parts = [e.reshape(2, qblocks, 1, SUB, width) for e in ends]
    both = jnp.concatenate(parts, axis=2).reshape(2, qblocks, 2 * SUB, width).astype(BF16)
    for qb in range(qblocks):
        for r in (0, 1):
            start = pl.multiple_of(m * 4 * SUB + r * 2 * SUB, 2 * SUB)
            held[qb, pl.ds(start, 2 * SUB), :] = both[r, qb]


def signs(shape, share):
    lane = lax.broadcasted_iota(jnp.int32, shape, 1)
    return lane < share


def swap(x, share):
    return jnp.concatenate([x[:, share:], x[:, :share]], axis=1)


def taps_kernel(core, recv, first, mid, back, last, spec, keep, send, rows_held, held):
    groups, _, width = recv.shape
    share = width // 2
    prow = mid.shape[0]
    qlen = mid.shape[1] // 2
    qblocks = qlen // SUB
    each = prow // groups * SUB

    def load(qb):
        return recv[:, qb * each : (qb + 1) * each, :].reshape(groups * each, width)

    stage_one(first, load, prow, qblocks, rows_held)
    low = signs((qlen, width), share)

    def step(m, carry):
        ends = []
        for e in (0, 1):
            k1 = 2 * m + e
            rows = rows_held[pl.ds(2 * k1, 2)].reshape(2 * qlen, width)
            full = dot(mid[k1], rows)
            spec[k1] = full.astype(BF16)
            re, im = full[:qlen], full[qlen:]
            ore, oim = swap(re, share), swap(im, share)
            tre = re * ore + im * oim
            tim = im * ore - re * oim
            tim = jnp.where(low, -tim, tim)
            both = jnp.concatenate([tre, tim], axis=0).astype(BF16)
            ends.append(dot(back[k1], both))
        store_pair(ends, m, qblocks, held)
        return carry

    lax.fori_loop(0, prow // 2, step, 0, unroll=4)
    blocks = prow // groups
    flip = core[0] == 0
    low_tile = signs((SUB, width), share)
    for qb in range(0, qblocks, 2):
        halves = [[], []]
        for e in (0, 1):
            seq = dot(last[...], held[qb + e]).reshape(groups, blocks, SUB, width)
            for c in (0, 1):
                halves[c].append(jnp.where(low_tile, seq[:, 2 * c], seq[:, 2 * c + 1]))
        a, b = [jnp.concatenate(h, axis=1) for h in halves]
        rows = slice(qb * SUB, (qb + 2) * SUB)
        keep[:, rows, :] = jnp.where(flip, a, b).astype(BF16)
        send[:, rows, :] = jnp.where(flip, b, a).astype(BF16)


def main_kernel(core, recv, other, spec, first, mid, back, last, out, taps_held, rows_held, held):
    groups, full_rows, width = recv.shape
    share = width // 2
    prow = mid.shape[0]
    qlen = mid.shape[1] // 2
    qblocks = qlen // SUB
    blocks = prow // groups
    each = blocks * SUB
    tok = blocks * qlen
    flip = core[0] == 0

    def unpack(i, carry):
        mine = recv[i, tok:, :].astype(F32)
        theirs = other[i].astype(F32)
        for c in (0, 1):
            x = jnp.where(flip == (c == 0), mine, theirs)
            lo, hi = x[:, :share], x[:, share:]
            ends = [
                jnp.concatenate([h, h], axis=1).reshape(qblocks, 1, SUB, width) for h in (lo, hi)
            ]
            both = jnp.concatenate(ends, axis=1).reshape(qblocks, 2 * SUB, width).astype(BF16)
            for qb in range(qblocks):
                start = pl.multiple_of(i * each + c * 2 * SUB, 2 * SUB)
                taps_held[qb, pl.ds(start, 2 * SUB), :] = both[qb]
        return carry

    lax.fori_loop(0, groups, unpack, 0, unroll=8)
    stage_one(first, lambda qb: taps_held[qb], prow, qblocks, rows_held)
    low = signs((qlen, width), share)

    def step(m, carry):
        ends = []
        for e in (0, 1):
            k1 = 2 * m + e
            rows = rows_held[pl.ds(2 * k1, 2)].reshape(2 * qlen, width)
            filt = dot(mid[k1], rows)
            hre, him = filt[:qlen], filt[qlen:]
            him = jnp.where(low, him, -him)
            sig = spec[k1].astype(F32)
            re, im = sig[:qlen], sig[qlen:]
            both = jnp.concatenate([re * hre - im * him, re * him + im * hre], axis=0)
            ends.append(dot(back[k1], both.astype(BF16)))
        store_pair(ends, m, qblocks, held)
        return carry

    lax.fori_loop(0, prow // 2, step, 0, unroll=4)
    for qb in range(qblocks):
        seq = dot(last[...], held[qb]).reshape(groups, each, width)
        out[:, qb * each : (qb + 1) * each, :] = seq.astype(BF16)


def add_kernel(a, b, out):
    out[...] = (a[...].astype(F32) + b[...].astype(F32)).astype(BF16)


def join_kernel(a, b, whole, out):
    total = (a[...].astype(F32) + b[...].astype(F32)).astype(BF16)
    out[...] = total


def post_kernel(live, recv, key, value, cot, gate_out, key_out, value_out):
    groups, _, width = recv.shape
    share = width // 2
    blocks = live.shape[1]
    tok = key.shape[1]
    qlen = tok // blocks
    qblocks = qlen // SUB
    parts = [
        recv[j, :tok, :].astype(F32).reshape(qblocks, blocks, SUB, width) for j in range(groups)
    ]
    for p in range(blocks):
        rows = slice(p * qlen, (p + 1) * qlen)
        alive = live[0, p].astype(F32)
        mine = [x[:, p].reshape(qlen, width) for x in parts]
        conv = jnp.concatenate([x[:, :share] for x in mine], axis=1)
        grad = jnp.concatenate([x[:, share:] for x in mine], axis=1)
        gate_out[0, rows, :] = (cot[0, rows, :].astype(F32) * conv).astype(BF16)
        key_out[0, rows, :] = (grad * value[0, rows, :].astype(F32) * alive).astype(BF16)
        value_out[0, rows, :] = (grad * key[0, rows, :].astype(F32) * alive).astype(BF16)


def finish_kernel(scale, core, mine, theirs, out):
    groups, qlen, width = mine.shape
    share = width // 2
    flip = core[0] == 0
    a = mine[...].astype(F32) * scale
    b = theirs[...].astype(F32) * scale
    for c in (0, 1):
        x = jnp.where(flip == (c == 0), a, b)
        for e in (0, 1):
            row = jnp.concatenate(
                [x[j][:, e * share : (e + 1) * share] for j in range(groups)], axis=1
            )
            start = (2 * c + e) * qlen
            out[start : start + qlen, :] = row.astype(BF16)


SMEM = pl.BlockSpec(memory_space=pltpu.SMEM)
VM = pl.BlockSpec(memory_space=pltpu.VMEM)


def call(kernel, ins, outs, scratch=(), aliases=None, smem=0, name=None, flops=0, out_specs=None, in_specs=None):
    nbytes = sum(math.prod(x.shape) * 2 for x in ins) + sum(math.prod(x.shape) * 2 for x in outs)
    return pl.pallas_call(
        kernel,
        out_shape=outs if len(outs) > 1 else outs[0],
        in_specs=in_specs or ([SMEM] * smem + [VM] * (len(ins) - smem)),
        out_specs=out_specs or ([VM] * len(outs) if len(outs) > 1 else VM),
        scratch_shapes=list(scratch),
        input_output_aliases=aliases or {},
        compiler_params=pltpu.CompilerParams(vmem_limit_bytes=VMEM),
        cost_estimate=pl.CostEstimate(flops=flops, bytes_accessed=nbytes, transcendentals=0),
        name=name,
    )(*ins)


def shaped(shape, dtype=BF16):
    return jax.ShapeDtypeStruct(shape, dtype)


def local(out_gate, key_gate, value_input, filter_taps, cotangent, block_live):
    ctx = lax.axis_size("ctx")
    dp = lax.axis_size("dp")
    tok, chans = key_gate.shape[1:]
    blocks = block_live.shape[1]
    qlen = tok // blocks
    prow = blocks * ctx
    share = chans // ctx
    width = 2 * share
    qblocks = qlen // SUB
    tables = [jnp.asarray(t) for t in transform_tables(prow, qlen)]
    core = (lax.axis_index("dp") % 2).astype(jnp.int32).reshape(1)

    def trade(x, bit):
        return lax.ppermute(x, "dp", [(i, i ^ bit) for i in range(dp)])

    packed = call(
        prep_kernel,
        [core, block_live, out_gate, key_gate, value_input, cotangent, filter_taps],
        [shaped((ctx, tok + qlen, width))],
        smem=2,
        name="gate_and_pack",
    )
    recv = lax.all_to_all(packed, "ctx", split_axis=0, concat_axis=0, tiled=True)
    other_taps = trade(recv[:, tok:, :], 1)
    spec, keep, send = call(
        taps_kernel,
        [core, recv, *tables],
        [shaped((prow, 2 * qlen, width))] + [shaped((ctx, qlen, width))] * 2,
        scratch=[
            pltpu.VMEM((2 * prow, qlen, width), BF16),
            pltpu.VMEM((qblocks, 2 * prow * SUB, width), BF16),
        ],
        smem=1,
        name="taps_gradient",
    )
    got = trade(send, 1)
    outs = call(
        main_kernel,
        [core, recv, other_taps, spec, *tables],
        [shaped((ctx, tok + qlen, width))],
        scratch=[
            pltpu.VMEM((qblocks, prow * SUB, width), BF16),
            pltpu.VMEM((2 * prow, qlen, width), BF16),
            pltpu.VMEM((qblocks, 2 * prow * SUB, width), BF16),
        ],
        smem=1,
        name="convolve",
    )
    total = call(add_kernel, [keep, got], [shaped(keep.shape)], name="add_core")
    bit = 2
    while bit < dp:
        got = trade(total, bit)
        bit *= 2
        if bit < dp:
            total = call(add_kernel, [total, got], [shaped(keep.shape)], name="add_chip")
    summed = (total.astype(F32) + got.astype(F32)).astype(BF16)
    back = lax.dynamic_update_slice(outs, summed, (0, tok, 0))
    recv = lax.all_to_all(back, "ctx", split_axis=0, concat_axis=0, tiled=True)
    mine = recv[:, tok:, :]
    theirs = trade(mine, 1)
    grads = call(
        post_kernel,
        [block_live, recv, key_gate, value_input, cotangent],
        [shaped(key_gate.shape)] * 3,
        smem=1,
        name="ungate",
    )
    scale = 1.0 / math.sqrt(dp * tok * ctx)
    grad_taps = call(
        functools.partial(finish_kernel, scale),
        [core, mine, theirs],
        [shaped(filter_taps.shape)],
        smem=1,
        name="scale_taps",
    )
    return (*grads, grad_taps)


def solution(mesh):
    return jax.shard_map(
        local,
        mesh=mesh,
        in_specs=(
            P("dp", "ctx", None),
            P("dp", "ctx", None),
            P("dp", "ctx", None),
            P("ctx", None),
            P("dp", "ctx", None),
            P("dp", "ctx"),
        ),
        out_specs=(
            P("dp", "ctx", None),
            P("dp", "ctx", None),
            P("dp", "ctx", None),
            P("ctx", None),
        ),
        check_vma=False,
    )
```

time: 288 us -> 74.8 us (0.26)
  waiting for transfers between devices: 200 us -> 0.07 us
  blocking collectives: 0 us -> 46.5 us
  starting transfers between devices: 32.7 us -> 2.16 us
  Pallas kernels: 0 us -> 20.7 us
  matrix products: 15.6 us -> 0 us
  local copies, waits for them, and re-layouts: 18.2 us -> 3.61 us
  between operations: 14.4 us -> 0.69 us
  other arithmetic: 6.83 us -> 0.7 us
    all_to_all x8 -> x0, waiting for transfers between devices: 169 us -> none  [the longest x2 67.4 us: inverse_transform(): lax.all_to_all(twisted, 'ctx', split_axis=3, concat_axis=2, tiled=True)]
    all_to_all x0 -> x2, blocking collectives: none -> 46.5 us  [the longest x1 25.1 us: local(): lax.all_to_all(packed, 'ctx', split_axis=0, concat_axis=0, tiled=True)]
    all_to_all x8 -> x0, starting transfers between devices: 32.7 us -> none  [the longest x2 10.8 us: forward_transform(): lax.all_to_all(signals, 'ctx', split_axis=2, concat_axis=1, tiled=True)]
    psum x1 -> x0, waiting for transfers between devices: 30.2 us -> none  [local(): lax.psum(taps_seq.reshape(tok_count, chan_count).astype(jnp.float32).asty...]
    pallas_call x0 -> x6, Pallas kernels: none -> 20.7 us  [call(): pl.pallas_call(kernel, out_shape=outs if len(outs) > 1 else outs[0], in_s...]
    dot_general x24 -> x0, matrix products: 15.6 us -> none  [the longest x2 2.63 us: forward_transform(): jnp.einsum('saqc,qk->sakc', imag_in, sin_cols, preferred_element_type=jnp...]
    another operation x6 -> x0, local copies, waits for them, and re-layouts: 9.42 us -> none  [the longest x2 4.08 us: forward_transform(): packed = jnp.stack([real_part, imag_part]).astype(jnp.bfloat16)]
    convert_element_type x6 -> x0, other arithmetic: 4.67 us -> none  [the longest x1 1.7 us: local(): grad_taps = (taps_sum * scale_factor).astype(jnp.bfloat16)]
  transfers between devices with their start and end apart: 9 -> 4, of which waited for: 9 -> 1; matrix products, arithmetic and copies ran while one was open for 9% -> 1% of each run, Pallas kernels for 0% -> 14%
where the time goes in v1:
time: 74.8 us; the launch traced here: 74.4 us
  blocking collectives  46.5 us (62%)
  Pallas kernels  20.7 us (28%)
  local copies, waits for them, and re-layouts  3.61 us (5%)
  starting transfers between devices  2.16 us (3%)
    all_to_all x1, blocking collectives, local(): lax.all_to_all(packed, 'ctx', split_axis=0, concat_axis=0, tiled=True)  25.1 us
    all_to_all x1, blocking collectives, local(): recv = lax.all_to_all(back, 'ctx', split_axis=0, concat_axis=0, tiled=True)  21.4 us
    pallas_call x6, Pallas kernels, call(): pl.pallas_call(kernel, out_shape=outs if len(outs) > 1 else outs[0], in_s...  20.7 us
    unnamed x12, local copies, waits for them, and re-layouts  2.69 us
    ppermute x4, starting transfers between devices, trade(): return lax.ppermute(x, 'dp', [(i, i ^ bit) for i in range(dp)])  2.16 us
  transfers between devices with their start and end apart: 4, of which 1 were waited for; matrix products, arithmetic and copies ran while one was open for 1% of the time, Pallas kernels for 14%

profile of v1, /device:TPU:0, one launch (start us, length us, event | category | flops | bytes accessed | tf_op | source)
XLA Modules:
  0.0 74.4 jit_solution(4995239302222287439)
XLA Ops:
  0.6 2.4 %gate_and_pack.1 = bf16[8,320,128]{2,1,0:T(8,128)(2,1)} custom-call(s32[1]{0:T(128)} %bitcast.core, s32[1,4]{1,0:T(1,128)} %live.3, bf16[1,256,512]{2,1,0:T(8,128)(2,1)} %out_gate.1, bf16[1,256,512]{2,1,0:T(8,128)(2,1)} %key.3, bf16[1,256,512]{2,1,0:T(8,128)(2,1)} %value.3, bf16[1,256,512]{2,1,0:T(8,128)(2,1)} %cot.3, bf16[256,512]{1,0:T(8,128)(2,1)} %taps.1), custom_call_target="tpu_custom_call" | custom-call | bytes 1966090 | tf_op jit(solution)/shard_map/gate_and_pack/pallas_call | solution.py:259
  3.1 25.1 %all_to_all.10.recv = bf16[8,320,128]{2,1,0:T(8,128)(2,1)} all-to-all(bf16[8,320,128]{2,1,0:T(8,128)(2,1)} %gate_and_pack.1), channel_id=1, replica_groups=mesh['dp'=4,'ctx'=8] {'ctx'}, dimensions={0} | all-to-all | bytes 1310720 | tf_op jit(solution)/shard_map/all_to_all | solution.py:299
  28.1 5.9 %taps_gradient.1 = (bf16[32,128,128]{2,1,0:T(8,128)(2,1)}, bf16[8,64,128]{2,1,0:T(8,128)(2,1)}, bf16[8,64,128]{2,1,0:T(8,128)(2,1)}) custom-call(s32[1]{0:T(128)} %bitcast.core, bf16[8,320,128]{2,1,0:T(8,128)(2,1)} %all_to_all.10.recv, bf16[512,256]{1,0:T(8,128)(2,1)} %constant.29.clone.first, bf16[32,128,128]{2,1,0:T(8,128)(2,1)} %constant.30.clone.mid, ...), custom_call_target="tpu_custom_call" | custom-call | bytes 4587522 | tf_op jit(solution)/shard_map/taps_gradient/pallas_call | solution.py:259
  34.0 0.0 collective-permute-start.1
  34.0 0.9 %slice.8 = bf16[8,64,128]{2,1,0:T(8,128)(2,1)S(1)} slice(bf16[8,320,128]{2,1,0:T(8,128)(2,1)} %all_to_all.10.recv), slice={[0:8], [256:320], [0:128]} | slice | bytes 262144 | tf_op jit(solution)/shard_map/slice | solution.py:300
  35.0 0.6 collective-permute-start
  35.5 0.1 collective-permute-done.1.b
  35.6 0.0 copy-start.3
  35.6 0.7 copy-done.3
  36.3 1.7 %add_core.1 = bf16[8,64,128]{2,1,0:T(8,128)(2,1)} custom-call(bf16[8,64,128]{2,1,0:T(8,128)(2,1)} %get-tuple-element.11.a, bf16[8,64,128]{2,1,0:T(8,128)(2,1)} %copy-done.3), custom_call_target="tpu_custom_call" | custom-call | bytes 393216 | tf_op jit(solution)/shard_map/add_core/pallas_call | solution.py:259
  37.9 1.5 %collective-permute-start.2 = (bf16[8,64,128]{2,1,0:T(8,128)(2,1)}, bf16[8,64,128]{2,1,0:T(8,128)(2,1)S(1)}, u32[]{:S(2)}, u32[]{:S(2)}) collective-permute-start(bf16[8,64,128]{2,1,0:T(8,128)(2,1)} %add_core.1), channel_id=1, source_target_pairs={{0,16},{8,24},{16,0},{24,8},{1,17},{9,25},{17,1},{25,9},{2,18},{10... | collective-permute-start | bytes 393224 | tf_op jit(solution)/shard_map/ppermute | solution.py:290
  39.4 0.0 collective-permute-done.other
  39.4 0.0 copy-start.5
  39.4 0.7 copy-done.5
  40.1 0.0 copy-start.1
  40.1 6.3 %convolve.1 = bf16[8,320,128]{2,1,0:T(8,128)(2,1)} custom-call(s32[1]{0:T(128)} %bitcast.core, bf16[8,320,128]{2,1,0:T(8,128)(2,1)} %all_to_all.10.recv, bf16[8,64,128]{2,1,0:T(8,128)(2,1)} %copy-done.5, bf16[32,128,128]{2,1,0:T(8,128)(2,1)} %get-tuple-element.10.spec, bf16[512,256]{1,0:T(8,128)(2,1)} %constant.29.clone.first, ...), custom_call_target="tpu_custom_call" | custom-call | bytes 5111810 | tf_op jit(solution)/shard_map/convolve/pallas_call | solution.py:259
  46.4 0.0 collective-permute-done.2
  46.4 0.0 copy-done.1
  46.4 0.7 fusion
  47.1 21.4 %all_to_all.11.recv = bf16[8,320,128]{2,1,0:T(8,128)(2,1)S(1)} all-to-all(bf16[8,320,128]{2,1,0:T(8,128)(2,1)} %fusion), channel_id=1, replica_groups=mesh['dp'=4,'ctx'=8] {'ctx'}, dimensions={0} | all-to-all | bytes 1310720 | tf_op jit(solution)/shard_map/all_to_all | solution.py:334
  68.5 0.0 copy-start
  68.5 0.0 copy-start.2
  68.5 0.1 collective-permute-start.3
  68.6 0.7 copy-done
  69.4 2.5 %ungate.1 = (bf16[1,256,512]{2,1,0:T(8,128)(2,1)}, bf16[1,256,512]{2,1,0:T(8,128)(2,1)}, bf16[1,256,512]{2,1,0:T(8,128)(2,1)}) custom-call(s32[1,4]{1,0:T(1,128)} %live.3, bf16[8,320,128]{2,1,0:T(8,128)(2,1)} %copy-done, bf16[1,256,512]{2,1,0:T(8,128)(2,1)} %key.3, bf16[1,256,512]{2,1,0:T(8,128)(2,1)} %value.3, bf16[1,256,512]{2,1,0:T(8,128)(2,1)} %cot.3), custom_call_target="tpu_custom_call" | custom-call | bytes 2228232 | tf_op jit(solution)/shard_map/ungate/pallas_call | solution.py:259
  71.9 0.0 copy-done.2
  71.9 0.0 collective-permute-done.3.theirs
  71.9 0.0 copy-start.4
  71.9 0.6 copy-done.4
  72.5 1.8 %scale_taps.1 = bf16[256,512]{1,0:T(8,128)(2,1)} custom-call(s32[1]{0:T(128)} %bitcast.core, bf16[8,64,128]{2,1,0:T(8,128)(2,1)} %copy-done.2, bf16[8,64,128]{2,1,0:T(8,128)(2,1)} %copy-done.4), custom_call_target="tpu_custom_call" | custom-call | bytes 524290 | tf_op jit(solution)/shard_map/scale_taps/pallas_call | solution.py:259
  (1 shorter events, 0.0 us)
Async XLA Ops:
  34.0 1.6 %collective-permute-start.1 = (bf16[8,64,128]{2,1,0:T(8,128)(2,1)}, bf16[8,64,128]{2,1,0:T(8,128)(2,1)S(1)}, u32[]{:S(2)}, u32[]{:S(2)}) collective-permute-start(bf16[8,64,128]{2,1,0:T(8,128)(2,1)} %get-tuple-element.12), channel_id=1, source_target_pairs={{0,8},{8,0},{16,24},{24,16},{1,9},{9,1},{17,25},{25,17},{2,10},{10... | collective-permute-start | bytes 393224 | tf_op jit(solution)/shard_map/ppermute | solution.py:290
  35.0 4.5 %collective-permute-start = (bf16[8,64,128]{2,1,0:T(8,128)(2,1)S(1)}, bf16[8,64,128]{2,1,0:T(8,128)(2,1)S(1)}, u32[]{:S(2)}, u32[]{:S(2)}) collective-permute-start(bf16[8,64,128]{2,1,0:T(8,128)(2,1)S(1)} %slice.8), channel_id=1, source_target_pairs={{0,8},{8,0},{16,24},{24,16},{1,9},{9,1},{17,25},{25,17},{2,10},{10... | collective-permute-start | bytes 393224 | tf_op jit(solution)/shard_map/ppermute | solution.py:290
  35.6 0.7 copy-start.3
  37.9 8.5 %collective-permute-start.2 = (bf16[8,64,128]{2,1,0:T(8,128)(2,1)}, bf16[8,64,128]{2,1,0:T(8,128)(2,1)S(1)}, u32[]{:S(2)}, u32[]{:S(2)}) collective-permute-start(bf16[8,64,128]{2,1,0:T(8,128)(2,1)} %add_core.1), channel_id=1, source_target_pairs={{0,16},{8,24},{16,0},{24,8},{1,17},{9,25},{17,1},{25,9},{2,18},{10... | collective-permute-start | bytes 393224 | tf_op jit(solution)/shard_map/ppermute | solution.py:290
  39.4 0.7 copy-start.5
  40.1 6.3 %copy-start.1 = (bf16[8,64,128]{2,1,0:T(8,128)(2,1)S(1)}, bf16[8,64,128]{2,1,0:T(8,128)(2,1)}, u32[]{:S(2)}) copy-start(bf16[8,64,128]{2,1,0:T(8,128)(2,1)} %add_core.1) | copy-start | bytes 393220
  68.5 0.8 %copy-start = (bf16[8,320,128]{2,1,0:T(8,128)(2,1)}, bf16[8,320,128]{2,1,0:T(8,128)(2,1)S(1)}, u32[]{:S(2)}) copy-start(bf16[8,320,128]{2,1,0:T(8,128)(2,1)S(1)} %all_to_all.11.recv) | copy-start | bytes 1966084
  68.5 3.4 %copy-start.2 = (bf16[8,64,128]{2,1,0:T(8,128)(2,1)}, bf16[8,64,128]{2,1,0:T(8,128)(2,1)S(1)}, u32[]{:S(2)}) copy-start(bf16[8,64,128]{2,1,0:T(8,128)(2,1)S(1)} %slice.9.mine) | copy-start | bytes 393220
  68.5 3.4 %collective-permute-start.3 = (bf16[8,64,128]{2,1,0:T(8,128)(2,1)S(1)}, bf16[8,64,128]{2,1,0:T(8,128)(2,1)S(1)}, u32[]{:S(2)}, u32[]{:S(2)}) collective-permute-start(bf16[8,64,128]{2,1,0:T(8,128)(2,1)S(1)} %slice.9.mine), channel_id=1, source_target_pairs={{0,8},{8,0},{16,24},{24,16},{1,9},{9,1},{17,25},{25,17},{2,10},{10... | collective-permute-start | bytes 393224 | tf_op jit(solution)/shard_map/ppermute | solution.py:290
  71.9 0.6 copy-start.4

commit v2 on v1

--- a/solution.py
+++ b/solution.py
@@ -12,7 +12,7 @@
 
 
 SUB = 8
-VMEM = 60 * 1024 * 1024
+SPARE = 4 * 1024 * 1024
 F32 = jnp.float32
 BF16 = jnp.bfloat16
 
@@ -44,20 +44,53 @@
     return jnp.dot(a, b, preferred_element_type=F32)
 
 
-def prep_kernel(core, live, out_gate, key, value, cot, taps, out):
+def core_place():
+    return lax.rem(lax.axis_index("dp"), 2)
+
+
+def prep_kernel(
+    live_far, out_gate_far, key_far, value_far, cot_far, taps_far,
+    out, key_out, value_out, cot, key, value, out_gate, taps, live, sems,
+):
+    core = core_place()
     groups = out.shape[0]
     share = out.shape[2] // 2
     blocks = live.shape[1]
-    tok = key.shape[1]
+    tok = key.shape[0]
     qlen = tok // blocks
     qblocks = qlen // SUB
+    copies = []
     for p in range(0, blocks, 2):
+        rows = slice(p * qlen, (p + 2) * qlen)
+        copies.append([
+            pltpu.make_async_copy(far.at[0, rows], near.at[rows], sems.at[2 * p + i])
+            for i, (far, near) in enumerate(
+                [(key_far, key), (value_far, value), (cot_far, cot), (out_gate_far, out_gate)]
+            )
+        ])
+    half = tok // 2
+    taps_copy = pltpu.make_async_copy(
+        taps_far.at[pl.ds(pl.multiple_of(core * half, half), half)], taps, sems.at[2 * blocks]
+    )
+    live_copy = pltpu.make_async_copy(live_far, live, sems.at[2 * blocks + 1])
+    live_copy.start()
+    for group in copies:
+        for copy in group:
+            copy.start()
+    taps_copy.start()
+    live_copy.wait()
+    for p in range(0, blocks, 2):
+        for copy in copies[p // 2]:
+            copy.wait()
         pair = []
         for e in (0, 1):
             rows = slice((p + e) * qlen, (p + e + 1) * qlen)
             alive = live[0, p + e].astype(F32)
-            u = key[0, rows, :].astype(F32) * value[0, rows, :].astype(F32) * alive
-            g = cot[0, rows, :].astype(F32) * out_gate[0, rows, :].astype(F32)
+            kept = key[rows, :].astype(F32) * alive
+            u = kept * value[rows, :].astype(F32)
+            key_out[rows, :] = kept.astype(BF16)
+            value_out[rows, :] = (value[rows, :].astype(F32) * alive).astype(BF16)
+            g = cot[rows, :].astype(F32) * out_gate[rows, :].astype(F32)
             pair.append((u, g))
         for j in range(groups):
             lanes = slice(j * share, (j + 1) * share)
@@ -69,8 +102,8 @@
             for qb in range(qblocks):
                 start = qb * blocks * SUB + p * SUB
                 out[j, start : start + 2 * SUB, :] = both[qb]
-    half = tok // 2
-    mine = taps[pl.ds(pl.multiple_of(core[0] * half, half), half), :].astype(F32)
+    taps_copy.wait()
+    mine = taps[...].astype(F32)
     for j in range(groups):
         lanes = slice(j * share, (j + 1) * share)
         both = jnp.concatenate([mine[:qlen, lanes], mine[qlen:, lanes]], axis=1)
@@ -106,7 +139,7 @@
     return jnp.concatenate([x[:, share:], x[:, :share]], axis=1)
 
 
-def taps_kernel(core, recv, first, mid, back, last, spec, keep, send, rows_held, held):
+def taps_kernel(recv, first, mid, back, last, spec, keep, send, rows_held, held):
     groups, _, width = recv.shape
     share = width // 2
     prow = mid.shape[0]
@@ -139,7 +172,7 @@
 
     lax.fori_loop(0, prow // 2, step, 0, unroll=4)
     blocks = prow // groups
-    flip = core[0] == 0
+    flip = core_place() == 0
     low_tile = signs((SUB, width), share)
     for qb in range(0, qblocks, 2):
         halves = [[], []]
@@ -153,7 +186,7 @@
         send[:, rows, :] = jnp.where(flip, b, a).astype(BF16)
 
 
-def main_kernel(core, recv, other, spec, first, mid, back, last, out, taps_held, rows_held, held):
+def main_kernel(recv, other, spec, first, mid, back, last, out, taps_held, rows_held, held):
     groups, full_rows, width = recv.shape
     share = width // 2
     prow = mid.shape[0]
@@ -162,7 +195,7 @@
     blocks = prow // groups
     each = blocks * SUB
     tok = blocks * qlen
-    flip = core[0] == 0
+    flip = core_place() == 0
 
     def unpack(i, carry):
         mine = recv[i, tok:, :].astype(F32)
@@ -208,36 +241,41 @@
     out[...] = (a[...].astype(F32) + b[...].astype(F32)).astype(BF16)
 
 
-def join_kernel(a, b, whole, out):
-    total = (a[...].astype(F32) + b[...].astype(F32)).astype(BF16)
-    out[...] = total
-
-
-def post_kernel(live, recv, key, value, cot, gate_out, key_out, value_out):
+def post_kernel(
+    recv, key, value, cot, gate_far, key_far, value_far, gate_out, key_out, value_out, sems
+):
     groups, _, width = recv.shape
     share = width // 2
-    blocks = live.shape[1]
-    tok = key.shape[1]
-    qlen = tok // blocks
+    tok = key.shape[0]
+    qlen = recv.shape[1] - tok
+    blocks = tok // qlen
     qblocks = qlen // SUB
     parts = [
         recv[j, :tok, :].astype(F32).reshape(qblocks, blocks, SUB, width) for j in range(groups)
     ]
+    copies = []
     for p in range(blocks):
         rows = slice(p * qlen, (p + 1) * qlen)
-        alive = live[0, p].astype(F32)
         mine = [x[:, p].reshape(qlen, width) for x in parts]
         conv = jnp.concatenate([x[:, :share] for x in mine], axis=1)
         grad = jnp.concatenate([x[:, share:] for x in mine], axis=1)
-        gate_out[0, rows, :] = (cot[0, rows, :].astype(F32) * conv).astype(BF16)
-        key_out[0, rows, :] = (grad * value[0, rows, :].astype(F32) * alive).astype(BF16)
-        value_out[0, rows, :] = (grad * key[0, rows, :].astype(F32) * alive).astype(BF16)
-
-
-def finish_kernel(scale, core, mine, theirs, out):
+        gate_out[rows, :] = (cot[rows, :].astype(F32) * conv).astype(BF16)
+        key_out[rows, :] = (grad * value[rows, :].astype(F32)).astype(BF16)
+        value_out[rows, :] = (grad * key[rows, :].astype(F32)).astype(BF16)
+        for i, (near, far) in enumerate(
+            [(gate_out, gate_far), (key_out, key_far), (value_out, value_far)]
+        ):
+            copy = pltpu.make_async_copy(near.at[rows], far.at[0, rows], sems.at[3 * p + i])
+            copy.start()
+            copies.append(copy)
+    for copy in copies:
+        copy.wait()
+
+
+def finish_kernel(scale, mine, theirs, out):
     groups, qlen, width = mine.shape
     share = width // 2
-    flip = core[0] == 0
+    flip = core_place() == 0
     a = mine[...].astype(F32) * scale
     b = theirs[...].astype(F32) * scale
     for c in (0, 1):
@@ -250,20 +288,21 @@
             out[start : start + qlen, :] = row.astype(BF16)
 
 
-SMEM = pl.BlockSpec(memory_space=pltpu.SMEM)
 VM = pl.BlockSpec(memory_space=pltpu.VMEM)
-
-
-def call(kernel, ins, outs, scratch=(), aliases=None, smem=0, name=None, flops=0, out_specs=None, in_specs=None):
-    nbytes = sum(math.prod(x.shape) * 2 for x in ins) + sum(math.prod(x.shape) * 2 for x in outs)
+FAR = pl.BlockSpec(memory_space=pltpu.HBM)
+
+
+def call(kernel, ins, outs, scratch=(), aliases=None, name=None, flops=0, out_specs=None, in_specs=None):
+    nbytes = sum(math.prod(x.shape) * 2 for x in [*ins, *outs])
+    held = nbytes + sum(math.prod(x.shape) * 2 for x in scratch if x.dtype == BF16)
     return pl.pallas_call(
         kernel,
         out_shape=outs if len(outs) > 1 else outs[0],
-        in_specs=in_specs or ([SMEM] * smem + [VM] * (len(ins) - smem)),
+        in_specs=in_specs or ([VM] * len(ins)),
         out_specs=out_specs or ([VM] * len(outs) if len(outs) > 1 else VM),
         scratch_shapes=list(scratch),
         input_output_aliases=aliases or {},
-        compiler_params=pltpu.CompilerParams(vmem_limit_bytes=VMEM),
+        compiler_params=pltpu.CompilerParams(vmem_limit_bytes=held + SPARE),
         cost_estimate=pl.CostEstimate(flops=flops, bytes_accessed=nbytes, transcendentals=0),
         name=name,
     )(*ins)
@@ -284,42 +323,48 @@
     width = 2 * share
     qblocks = qlen // SUB
     tables = [jnp.asarray(t) for t in transform_tables(prow, qlen)]
-    core = (lax.axis_index("dp") % 2).astype(jnp.int32).reshape(1)
-
     def trade(x, bit):
         return lax.ppermute(x, "dp", [(i, i ^ bit) for i in range(dp)])
 
-    packed = call(
+    flat = (tok, chans)
+    packed, key, value, cot = call(
         prep_kernel,
-        [core, block_live, out_gate, key_gate, value_input, cotangent, filter_taps],
-        [shaped((ctx, tok + qlen, width))],
-        smem=2,
+        [
+            pltpu.with_memory_space_constraint(x, pltpu.HBM)
+            for x in (block_live, out_gate, key_gate, value_input, cotangent, filter_taps)
+        ],
+        [shaped((ctx, tok + qlen, width))] + [shaped(flat)] * 3,
+        scratch=[
+            *[pltpu.VMEM(flat, BF16)] * 3,
+            pltpu.VMEM((tok // 2, chans), BF16),
+            pltpu.SMEM(block_live.shape, jnp.int32),
+            pltpu.SemaphoreType.DMA((2 * blocks + 2,)),
+        ],
+        in_specs=[FAR] * 6,
         name="gate_and_pack",
     )
     recv = lax.all_to_all(packed, "ctx", split_axis=0, concat_axis=0, tiled=True)
     other_taps = trade(recv[:, tok:, :], 1)
     spec, keep, send = call(
         taps_kernel,
-        [core, recv, *tables],
+        [recv, *tables],
         [shaped((prow, 2 * qlen, width))] + [shaped((ctx, qlen, width))] * 2,
         scratch=[
             pltpu.VMEM((2 * prow, qlen, width), BF16),
             pltpu.VMEM((qblocks, 2 * prow * SUB, width), BF16),
         ],
-        smem=1,
         name="taps_gradient",
     )
     got = trade(send, 1)
     outs = call(
         main_kernel,
-        [core, recv, other_taps, spec, *tables],
+        [recv, other_taps, spec, *tables],
         [shaped((ctx, tok + qlen, width))],
         scratch=[
             pltpu.VMEM((qblocks, prow * SUB, width), BF16),
             pltpu.VMEM((2 * prow, qlen, width), BF16),
             pltpu.VMEM((qblocks, 2 * prow * SUB, width), BF16),
         ],
-        smem=1,
         name="convolve",
     )
     total = call(add_kernel, [keep, got], [shaped(keep.shape)], name="add_core")
@@ -336,17 +381,17 @@
     theirs = trade(mine, 1)
     grads = call(
         post_kernel,
-        [block_live, recv, key_gate, value_input, cotangent],
+        [recv, key, value, cot],
         [shaped(key_gate.shape)] * 3,
-        smem=1,
+        scratch=[pltpu.VMEM(flat, BF16)] * 3 + [pltpu.SemaphoreType.DMA((3 * blocks,))],
+        out_specs=[FAR] * 3,
         name="ungate",
     )
     scale = 1.0 / math.sqrt(dp * tok * ctx)
     grad_taps = call(
         functools.partial(finish_kernel, scale),
-        [core, mine, theirs],
+        [mine, theirs],
         [shaped(filter_taps.shape)],
-        smem=1,
         name="scale_taps",
     )
     return (*grads, grad_taps)

time: 74.8 us -> 60.6 us (0.81)
  Pallas kernels: 20.7 us -> 10.4 us
  local copies, waits for them, and re-layouts: 3.61 us -> 0.05 us
  waiting for transfers between devices: 0.07 us -> 1.81 us
  blocking collectives: 46.5 us -> 45.1 us
    pallas_call x6, Pallas kernels: 20.7 us -> 10.4 us  [call(): pl.pallas_call(kernel, out_shape=outs if len(outs) > 1 else outs[0], in_s...]
    unnamed x12 -> x8, local copies, waits for them, and re-layouts: 2.69 us -> 0.03 us
    ppermute x4, waiting for transfers between devices: 0.07 us -> 1.81 us  [trade(): return lax.ppermute(x, 'dp', [(i, i ^ bit) for i in range(dp)])]
    all_to_all x1, blocking collectives: 21.4 us -> 20.2 us  [local(): recv = lax.all_to_all(back, 'ctx', split_axis=0, concat_axis=0, tiled=True)]
    slice x1, local copies, waits for them, and re-layouts: 0.91 us -> 0.01 us  [local(): other_taps = trade(recv[:, tok:, :], 1)]
  transfers between devices with their start and end apart: 4 -> 4, of which waited for: 1 -> 3; matrix products, arithmetic and copies ran while one was open for 1% -> 0% of each run, Pallas kernels for 14% -> 7%
where the time goes in v2:
time: 60.6 us; the launch traced here: 60.4 us
  blocking collectives  45.1 us (74%)
  Pallas kernels  10.4 us (17%)
  starting transfers between devices  2.28 us (4%)
  waiting for transfers between devices  1.81 us (3%)
  between operations  0.74 us (1%)
    all_to_all x1, blocking collectives, local(): lax.all_to_all(packed, 'ctx', split_axis=0, concat_axis=0, tiled=True)  24.9 us
    all_to_all x1, blocking collectives, local(): recv = lax.all_to_all(back, 'ctx', split_axis=0, concat_axis=0, tiled=True)  20.2 us
    pallas_call x6, Pallas kernels, call(): pl.pallas_call(kernel, out_shape=outs if len(outs) > 1 else outs[0], in_s...  10.4 us
    ppermute x4, starting transfers between devices, trade(): return lax.ppermute(x, 'dp', [(i, i ^ bit) for i in range(dp)])  2.28 us
    ppermute x4, waiting for transfers between devices, trade(): return lax.ppermute(x, 'dp', [(i, i ^ bit) for i in range(dp)])  1.81 us
  transfers between devices with their start and end apart: 4, of which 3 were waited for; matrix products, arithmetic and copies ran while one was open for 0% of the time, Pallas kernels for 7%

profile of v2, /device:TPU:0, one launch (start us, length us, event | category | flops | bytes accessed | tf_op | source)
XLA Modules:
  0.0 60.4 jit_solution(13060564433194953909)
XLA Ops:
  0.6 0.0 copy-start
  0.6 0.0 copy-start.1
  0.7 1.8 %gate_and_pack.1 = (bf16[8,320,128]{2,1,0:T(8,128)(2,1)S(1)}, bf16[256,512]{1,0:T(8,128)(2,1)S(1)}, bf16[256,512]{1,0:T(8,128)(2,1)S(1)}, bf16[256,512]{1,0:T(8,128)(2,1)S(1)}) custom-call(s32[1,4]{1,0:T(1,128)} %live_far.1, bf16[1,256,512]{2,1,0:T(8,128)(2,1)} %out_gate_far.1, bf16[1,256,512]{2,1,0:T(8,128)(2,1)} %key_far.1, ...), custom_call_target="tpu_custom_call" | custom-call | bytes 2752520 | tf_op jit(solution)/shard_map/gate_and_pack/pallas_call | solution.py:298
  2.4 0.0 copy-start.2
  2.5 0.0 copy-start.3
  2.5 24.9 %all_to_all.10.recv = bf16[8,320,128]{2,1,0:T(8,128)(2,1)S(1)} all-to-all(bf16[8,320,128]{2,1,0:T(8,128)(2,1)S(1)} %get-tuple-element.14), channel_id=1, replica_groups=mesh['dp'=4,'ctx'=8] {'ctx'}, dimensions={0} | all-to-all | bytes 1310720 | tf_op jit(solution)/shard_map/all_to_all | solution.py:346
  27.4 0.0 copy-done
  27.4 0.0 copy-done.1
  27.4 0.0 copy-done.2
  27.4 0.0 copy-done.3
  27.4 3.4 %taps_gradient.1 = (bf16[32,128,128]{2,1,0:T(8,128)(2,1)S(1)}, bf16[8,64,128]{2,1,0:T(8,128)(2,1)S(1)}, bf16[8,64,128]{2,1,0:T(8,128)(2,1)S(1)}) custom-call(bf16[8,320,128]{2,1,0:T(8,128)(2,1)S(1)} %all_to_all.10.recv, bf16[512,256]{1,0:T(8,128)(2,1)S(1)} %copy-done.3, bf16[32,128,128]{2,1,0:T(8,128)(2,1)S(1)} %copy-done.1, ...), custom_call_target="tpu_custom_call" | custom-call | bytes 4587520 | tf_op jit(solution)/shard_map/taps_gradient/pallas_call | solution.py:298
  30.8 0.1 collective-permute-start.1
  30.9 0.6 collective-permute-start
  31.4 0.8 %collective-permute-done.1.b = bf16[8,64,128]{2,1,0:T(8,128)(2,1)S(1)} collective-permute-done((bf16[8,64,128]{2,1,0:T(8,128)(2,1)S(1)}, bf16[8,64,128]{2,1,0:T(8,128)(2,1)S(1)}, u32[]{:S(2)}, u32[]{:S(2)}) %collective-permute-start.1) | collective-permute-done | bytes 131104 | tf_op jit(solution)/shard_map/ppermute | solution.py:327
  32.2 1.6 %collective-permute-start.2 = (bf16[8,64,128]{2,1,0:T(8,128)(2,1)S(1)}, bf16[8,64,128]{2,1,0:T(8,128)(2,1)S(1)}, u32[]{:S(2)}, u32[]{:S(2)}) collective-permute-start(bf16[8,64,128]{2,1,0:T(8,128)(2,1)S(1)} %add_core.1), channel_id=1, source_target_pairs={{0,16},{8,24},{16,0},{24,8},{1,17},{9,25},{17,1},{25,9},{2,18},{10... | collective-permute-start | bytes 393224 | tf_op jit(solution)/shard_map/ppermute | solution.py:327
  33.8 0.0 collective-permute-done.other
  33.8 3.2 %convolve.1 = bf16[8,320,128]{2,1,0:T(8,128)(2,1)S(1)} custom-call(bf16[8,320,128]{2,1,0:T(8,128)(2,1)S(1)} %all_to_all.10.recv, bf16[8,64,128]{2,1,0:T(8,128)(2,1)S(1)} %collective-permute-done.other, bf16[32,128,128]{2,1,0:T(8,128)(2,1)S(1)} %get-tuple-element.15.spec, bf16[512,256]{1,0:T(8,128)(2,1)S(1)} %copy-done.3, ...), custom_call_target="tpu_custom_call" | custom-call | bytes 5111808 | tf_op jit(solution)/shard_map/convolve/pallas_call | solution.py:298
  37.0 0.8 %collective-permute-done.2 = bf16[8,64,128]{2,1,0:T(8,128)(2,1)S(1)} collective-permute-done((bf16[8,64,128]{2,1,0:T(8,128)(2,1)S(1)}, bf16[8,64,128]{2,1,0:T(8,128)(2,1)S(1)}, u32[]{:S(2)}, u32[]{:S(2)}) %collective-permute-start.2) | collective-permute-done | bytes 131104 | tf_op jit(solution)/shard_map/ppermute | solution.py:327
  37.8 0.1 fusion
  37.9 20.2 %all_to_all.11.recv = bf16[8,320,128]{2,1,0:T(8,128)(2,1)S(1)} all-to-all(bf16[8,320,128]{2,1,0:T(8,128)(2,1)S(1)} %fusion), channel_id=1, replica_groups=mesh['dp'=4,'ctx'=8] {'ctx'}, dimensions={0} | all-to-all | bytes 1310720 | tf_op jit(solution)/shard_map/all_to_all | solution.py:379
  58.1 0.1 collective-permute-start.3
  58.2 1.1 %ungate.1 = (bf16[1,256,512]{2,1,0:T(8,128)(2,1)}, bf16[1,256,512]{2,1,0:T(8,128)(2,1)}, bf16[1,256,512]{2,1,0:T(8,128)(2,1)}) custom-call(bf16[8,320,128]{2,1,0:T(8,128)(2,1)S(1)} %all_to_all.11.recv, bf16[256,512]{1,0:T(8,128)(2,1)S(1)} %get-tuple-element.18.key, bf16[256,512]{1,0:T(8,128)(2,1)S(1)} %get-tuple-element.19.value, ...), custom_call_target="tpu_custom_call" | custom-call | bytes 2228224 | tf_op jit(solution)/shard_map/ungate/pallas_call | solution.py:298
  59.3 0.2 collective-permute-done.3.theirs
  59.5 0.9 %scale_taps.1 = bf16[256,512]{1,0:T(8,128)(2,1)} custom-call(bf16[8,64,128]{2,1,0:T(8,128)(2,1)S(1)} %slice.9.mine, bf16[8,64,128]{2,1,0:T(8,128)(2,1)S(1)} %collective-permute-done.3.theirs), custom_call_target="tpu_custom_call" | custom-call | bytes 524288 | tf_op jit(solution)/shard_map/scale_taps/pallas_call | solution.py:298
  (3 shorter events, 0.1 us)
Async XLA Ops:
  0.6 26.7 %copy-start = (bf16[32,128,128]{2,1,0:T(8,128)(2,1)S(1)}, bf16[32,128,128]{2,1,0:T(8,128)(2,1)}, u32[]{:S(2)}) copy-start(bf16[32,128,128]{2,1,0:T(8,128)(2,1)} %constant.14.clone.back) | copy-start | bytes 3145732
  0.6 26.7 %copy-start.1 = (bf16[32,128,128]{2,1,0:T(8,128)(2,1)S(1)}, bf16[32,128,128]{2,1,0:T(8,128)(2,1)}, u32[]{:S(2)}) copy-start(bf16[32,128,128]{2,1,0:T(8,128)(2,1)} %constant.13.clone.mid) | copy-start | bytes 3145732
  2.4 24.9 %copy-start.2 = (bf16[256,512]{1,0:T(8,128)(2,1)S(1)}, bf16[256,512]{1,0:T(8,128)(2,1)}, u32[]{:S(2)}) copy-start(bf16[256,512]{1,0:T(8,128)(2,1)} %constant.15.clone.last) | copy-start | bytes 786436
  2.5 24.9 %copy-start.3 = (bf16[512,256]{1,0:T(8,128)(2,1)S(1)}, bf16[512,256]{1,0:T(8,128)(2,1)}, u32[]{:S(2)}) copy-start(bf16[512,256]{1,0:T(8,128)(2,1)} %constant.12.clone.first) | copy-start | bytes 786436
  30.8 1.4 %collective-permute-start.1 = (bf16[8,64,128]{2,1,0:T(8,128)(2,1)S(1)}, bf16[8,64,128]{2,1,0:T(8,128)(2,1)S(1)}, u32[]{:S(2)}, u32[]{:S(2)}) collective-permute-start(bf16[8,64,128]{2,1,0:T(8,128)(2,1)S(1)} %get-tuple-element.17), channel_id=1, source_target_pairs={{0,8},{8,0},{16,24},{24,16},{1,9},{9,1},{17,25},{25,17},{2,10},{10... | collective-permute-start | bytes 393224 | tf_op jit(solution)/shard_map/ppermute | solution.py:327
  30.9 2.9 %collective-permute-start = (bf16[8,64,128]{2,1,0:T(8,128)(2,1)S(1)}, bf16[8,64,128]{2,1,0:T(8,128)(2,1)S(1)}, u32[]{:S(2)}, u32[]{:S(2)}) collective-permute-start(bf16[8,64,128]{2,1,0:T(8,128)(2,1)S(1)} %slice.8), channel_id=1, source_target_pairs={{0,8},{8,0},{16,24},{24,16},{1,9},{9,1},{17,25},{25,17},{2,10},{10... | collective-permute-start | bytes 393224 | tf_op jit(solution)/shard_map/ppermute | solution.py:327
  32.2 5.6 %collective-permute-start.2 = (bf16[8,64,128]{2,1,0:T(8,128)(2,1)S(1)}, bf16[8,64,128]{2,1,0:T(8,128)(2,1)S(1)}, u32[]{:S(2)}, u32[]{:S(2)}) collective-permute-start(bf16[8,64,128]{2,1,0:T(8,128)(2,1)S(1)} %add_core.1), channel_id=1, source_target_pairs={{0,16},{8,24},{16,0},{24,8},{1,17},{9,25},{17,1},{25,9},{2,18},{10... | collective-permute-start | bytes 393224 | tf_op jit(solution)/shard_map/ppermute | solution.py:327
  58.1 1.4 %collective-permute-start.3 = (bf16[8,64,128]{2,1,0:T(8,128)(2,1)S(1)}, bf16[8,64,128]{2,1,0:T(8,128)(2,1)S(1)}, u32[]{:S(2)}, u32[]{:S(2)}) collective-permute-start(bf16[8,64,128]{2,1,0:T(8,128)(2,1)S(1)} %slice.9.mine), channel_id=1, source_target_pairs={{0,8},{8,0},{16,24},{24,16},{1,9},{9,1},{17,25},{25,17},{2,10},{10... | collective-permute-start | bytes 393224 | tf_op jit(solution)/shard_map/ppermute | solution.py:327

commit v3 on v2

v3 whole, which is shorter than its diff:
```python
import functools
import math

import jax
import jax.numpy as jnp
import ml_dtypes
import numpy as np
from jax import lax
from jax.experimental import pallas as pl
from jax.experimental.pallas import tpu as pltpu
from jax.sharding import PartitionSpec as P


SUB = 8
TEAM = 4
PIECES = 4
SPARE = 4 * 1024 * 1024
F32 = jnp.float32
BF16 = jnp.bfloat16


def transform_tables(prow, qlen):
    total = prow * qlen
    k1 = np.arange(prow)
    p = np.arange(prow)
    theta = 2.0 * np.pi * (((4 * k1[:, None] + 1) * p[None, :]) % (4 * prow)) / (4 * prow)
    eye = np.eye(SUB)
    first = np.stack([np.cos(theta), -np.sin(theta)], axis=1)
    first = np.einsum("krp,ab->krapb", first, eye).reshape(prow * 2 * SUB, prow * SUB)
    last = np.stack([np.cos(theta), -np.sin(theta)], axis=0) / total
    last = last.reshape(2, prow // 2, 2, prow)
    last = np.einsum("rmlp,ab->pamrlb", last, eye).reshape(prow * SUB, prow * 2 * SUB)
    q = np.arange(qlen)
    k2 = np.arange(qlen)
    phase = (4 * k1[:, None, None] + 1 + 4 * prow * k2[None, :, None]) * q[None, None, :]
    phi = 2.0 * np.pi * (phase % (4 * total)) / (4 * total)
    re, im = np.cos(phi), -np.sin(phi)
    mid = np.concatenate(
        [np.concatenate([re, -im], axis=2), np.concatenate([im, re], axis=2)], axis=1
    )
    back = np.swapaxes(mid, 1, 2)
    return [t.astype(ml_dtypes.bfloat16) for t in (first, mid, back, last)]


def spread_table(qblocks, copies, share):
    spread = np.einsum("ab,cd,e->acbed", np.eye(qblocks), np.eye(share), np.ones(copies))
    return spread.reshape(qblocks * share, -1).astype(ml_dtypes.bfloat16)


def dot(a, b):
    return jnp.dot(a, b, preferred_element_type=F32)


def turn(x, shift):
    width = x.shape[-1]
    shift %= width
    if width == 128:
        return pltpu.roll(x, shift, 1)
    return jnp.concatenate([x[:, width - shift :], x[:, : width - shift]], axis=1)


def lanes_of(shape):
    return lax.broadcasted_iota(jnp.int32, shape, len(shape) - 1)


def regroup(groups, count, unit, load, store, hold, steps):
    for place, step in enumerate(steps):
        for g in range(groups):
            for a in range(count):
                if a & step:
                    continue
                pair = [
                    load(g, k) if place == 0 else hold[g * count + k] for k in (a, a + step)
                ]
                lane = lanes_of(pair[0].shape)
                low = (lane // (unit * step)) % 2 == 0
                x = jnp.where(low, pair[0], turn(pair[1], unit * step))
                y = jnp.where(low, turn(pair[0], -unit * step), pair[1])
                if place == len(steps) - 1:
                    store(g, a, a + step, x, y)
                else:
                    hold[g * count + a] = x
                    hold[g * count + a + step] = y


def gather_lanes(xs, unit):
    return [
        jnp.concatenate([x[:, k * unit : (k + 1) * unit] for x in xs], axis=1)
        for k in range(xs[0].shape[1] // unit)
    ]


def prep_kernel(
    team, live_far, out_gate_far, key_far, value_far, cot_far, taps_far,
    out, key_out, value_out, cot, key, value, out_gate, taps, live, hold, hold_taps, sems,
):
    blocks, qlen, chans = key.shape
    lanes = out.shape[2]
    share = lanes // (2 * blocks)
    span = min(chans, 128)
    per = span // share
    spans = chans // span
    place = lax.rem(lax.axis_index("dp"), team)
    parts = 2
    size = qlen // parts
    taps_copy = pltpu.make_async_copy(taps_far.at[place], taps, sems.at[0])
    live_copy = pltpu.make_async_copy(live_far, live, sems.at[1])
    copies = []
    for part in range(parts):
        rows = pl.ds(part * size, size)
        copies.append([
            pltpu.make_async_copy(far.at[:, rows], near.at[:, rows], sems.at[2 + 4 * part + i])
            for i, (far, near) in enumerate(
                [(key_far, key), (value_far, value), (cot_far, cot), (out_gate_far, out_gate)]
            )
        ])
    live_copy.start()
    for copy in copies[0]:
        copy.start()
    taps_copy.start()
    for group in copies[1:]:
        for copy in group:
            copy.start()
    live_copy.wait()

    def load(g, a):
        part, m = g // spans, g % spans
        if a == 0 and m == 0:
            for copy in copies[part]:
                copy.wait()
        p = a % blocks
        rows = slice(part * size, (part + 1) * size)
        cols = slice(m * span, (m + 1) * span)
        if a >= blocks:
            wide = cot[p, rows, cols].astype(F32)
            return (wide * out_gate[p, rows, cols].astype(F32)).astype(BF16)
        alive = live[0, p].astype(F32)
        kept = key[p, rows, cols].astype(F32) * alive
        wide = value[p, rows, cols].astype(F32)
        key_out[p, rows, cols] = kept.astype(BF16)
        value_out[p, rows, cols] = (wide * alive).astype(BF16)
        return (kept * wide).astype(BF16)

    def store(g, a, b, x, y):
        part, m = g // spans, g % spans
        rows = slice(part * size, (part + 1) * size)
        out[m * per + a, rows, :] = x
        out[m * per + b, rows, :] = y

    def load_taps(g, a):
        return taps[a * SUB : (a + 1) * SUB, g * span : (g + 1) * span].astype(F32)

    def store_taps(g, a, b, x, y):
        out[g * per + a, qlen:, :] = x.astype(BF16)
        out[g * per + b, qlen:, :] = y.astype(BF16)

    if lanes == span:
        regroup(parts * spans, 2 * blocks, share, load, store, hold, (1, 2, 4))
        taps_copy.wait()
        regroup(spans, qlen // SUB, share, load_taps, store_taps, hold_taps, (1, 2, 4))
    else:
        taps_copy.wait()
        for g in range(parts * spans):
            xs = gather_lanes([load(g, a) for a in range(2 * blocks)], share)
            for k in range(0, per, 2):
                store(g, k, k + 1, xs[k], xs[k + 1])
        for g in range(spans):
            xs = gather_lanes([load_taps(g, a) for a in range(qlen // SUB)], share)
            for k in range(0, per, 2):
                store_taps(g, k, k + 1, xs[k], xs[k + 1])


def pair_tiles(a, b, qblocks):
    width = a.shape[1]
    ends = [x.reshape(qblocks, 1, SUB, width) for x in (a, b)]
    return jnp.concatenate(ends, axis=1).reshape(qblocks, 2 * SUB, width).astype(BF16)


def main_kernel(
    recv, first, spread, turns, last,
    out, signal_held, taps_held, rows_held, held, hold, pre, post, taps_out,
):
    full_rows, width = recv.shape[1:]
    prow = turns.shape[0] // 2
    qlen = turns.shape[1] // 2
    qblocks = qlen // SUB
    team = qblocks // 2
    groups = recv.shape[0] // team
    blocks = prow // groups
    each = blocks * SUB
    share = width // qblocks

    for i in range(groups):
        for p in range(0, blocks, 2):
            rows = slice(i * each + p * SUB, i * each + (p + 2) * SUB)
            ends = [recv[(p + e) * groups + i, qlen:, :].astype(F32) for e in (0, 1)]
            taps_held[rows, :] = jnp.concatenate(ends, axis=0).astype(BF16)

    def load(i, b):
        return recv[b * groups + i, :qlen, :]

    def store(i, a, b, x, y):
        rows = slice(i * each + a * SUB, i * each + (a + 2) * SUB)
        signal_held[:, rows, :width] = pair_tiles(x.astype(F32), y.astype(F32), qblocks)

    regroup(groups, blocks, share, load, store, hold, (2, 1))
    for qb in range(qblocks):
        table = spread[:, qb * width : (qb + 1) * width]
        signal_held[qb, :, width:] = dot(taps_held[...], table).astype(BF16)
    for qb in range(0, qblocks, 2):
        ends = [
            dot(first[...], signal_held[qb + e]).reshape(2 * prow, SUB, 2 * width) for e in (0, 1)
        ]
        rows_held[:, qb * SUB : (qb + 2) * SUB, :] = jnp.concatenate(ends, axis=1).astype(BF16)

    low = lanes_of((qlen, width)) < width // 2

    def step(m, carry):
        ends = []
        for e in (0, 1):
            k1 = 2 * m + e
            rows = rows_held[pl.ds(2 * k1, 2)].reshape(2 * qlen, 2 * width)
            full = dot(turns[k1], rows)
            re, im = full[:qlen, :width], full[qlen:, :width]
            hre, him = full[:qlen, width:], full[qlen:, width:]
            him = jnp.where(low, him, -him)
            ore, oim = turn(re, width // 2), turn(im, width // 2)
            tim = im * ore - re * oim
            real = jnp.concatenate([re * hre - im * him, re * ore + im * oim], axis=1)
            imag = jnp.concatenate([re * him + im * hre, jnp.where(low, -tim, tim)], axis=1)
            both = jnp.concatenate([real, imag], axis=0).astype(BF16)
            ends.append(dot(turns[prow + k1], both))
        parts = [x.reshape(2, qblocks, 1, SUB, 2 * width) for x in ends]
        both = jnp.concatenate(parts, axis=2).reshape(2, qblocks, 2 * SUB, 2 * width).astype(BF16)
        for qb in range(qblocks):
            for r in (0, 1):
                start = pl.multiple_of(m * 4 * SUB + r * 2 * SUB, 2 * SUB)
                held[qb, pl.ds(start, 2 * SUB), :] = both[r, qb]
        return carry

    lax.fori_loop(0, prow // 2, step, 0, unroll=8)

    for qb in range(0, qblocks, 2):
        ends = []
        for e in (0, 1):
            seq = dot(last[...], held[qb + e])
            ends.append(seq[:, :width].reshape(groups, blocks, SUB, width))
            taps_out[qb + e] = seq[:, width:]
        for p in range(blocks):
            both = jnp.concatenate([x[:, p] for x in ends], axis=1).astype(BF16)
            pre[qb // 2 * blocks + p] = both.reshape(groups * 2 * SUB, width)

    def load_out(g, a):
        return pre[g * blocks + a]

    def store_out(g, a, b, x, y):
        rows = slice(g * 2 * SUB, (g + 1) * 2 * SUB)
        out[a * groups : (a + 1) * groups, rows, :] = x.reshape(groups, 2 * SUB, width)
        out[b * groups : (b + 1) * groups, rows, :] = y.reshape(groups, 2 * SUB, width)

    regroup(qblocks // 2, blocks, share, load_out, store_out, post, (1, 2))
    lane = lanes_of((each, width)) // share
    for i in range(groups):
        rows = slice(i * each, (i + 1) * each)
        xs = [taps_out[qb, rows, :] for qb in range(qblocks)]
        step = 1
        while step < team:
            low = (lane // step) % 2 == 0
            xs = [
                jnp.where(low, x, y) + turn(jnp.where(low, y, x), step * share)
                for x, y in zip(xs[::2], xs[1::2])
            ]
            step *= 2
        while len(xs) > 1:
            low = (lane // step) % 2 == 0
            xs = [jnp.where(low, x, y) for x, y in zip(xs[::2], xs[1::2])]
            step *= 2
        halves = xs[0].reshape(blocks // 2, 2 * SUB, width).astype(BF16)
        for b in range(team):
            out[b * groups + i, qlen:, :] = halves[b % 2]


def post_kernel(
    recv, key, value, cot, gate_far, key_far, value_far, gate_out, key_out, value_out, hold, sems
):
    blocks, qlen, chans = key.shape
    width = recv.shape[2]
    share = width // (2 * blocks)
    span = min(chans, 128)
    per = span // share
    spans = chans // span
    parts = 2
    size = qlen // parts
    copies = []

    def load(g, a):
        part, m = g // spans, g % spans
        return recv[m * per + a, part * size : (part + 1) * size, :]

    def store_one(g, a, x):
        part, m = g // spans, g % spans
        rows = slice(part * size, (part + 1) * size)
        cols = slice(m * span, (m + 1) * span)
        x = x.astype(F32)
        if a < blocks:
            gate_out[a, rows, cols] = (cot[a, rows, cols].astype(F32) * x).astype(BF16)
        else:
            p = a - blocks
            key_out[p, rows, cols] = (x * value[p, rows, cols].astype(F32)).astype(BF16)
            value_out[p, rows, cols] = (x * key[p, rows, cols].astype(F32)).astype(BF16)

    def store(g, a, b, x, y):
        store_one(g, a, x)
        store_one(g, b, y)
        if g % spans == spans - 1 and b == 2 * blocks - 1:
            part = g // spans
            rows = pl.ds(part * size, size)
            for i, (near, far) in enumerate(
                [(gate_out, gate_far), (key_out, key_far), (value_out, value_far)]
            ):
                copy = pltpu.make_async_copy(
                    near.at[:, rows], far.at[:, rows], sems.at[3 * part + i]
                )
                copy.start()
                copies.append(copy)

    if width == span:
        regroup(parts * spans, per, share, load, store, hold, (1, 2, 4))
    else:
        for g in range(parts * spans):
            xs = gather_lanes([load(g, a) for a in range(per)], share)
            for a in range(0, 2 * blocks, 2):
                store(g, a, a + 1, xs[a], xs[a + 1])
    for copy in copies:
        copy.wait()


def finish_kernel(scale, mine, theirs, out, hold):
    blocks, qlen, chans = out.shape
    width = mine.shape[2]
    share = width // (qlen // SUB)
    span = min(chans, 128)
    per = span // share
    spans = chans // span
    flip = lax.rem(lax.axis_index("dp"), 2) == 0

    def load(g, a):
        c, m = g // spans, g % spans
        x, y = mine[m * per + a], theirs[m * per + a]
        return jnp.where(flip == (c == 0), x, y)

    def store(g, a, b, x, y):
        c, m = g // spans, g % spans
        ends = [z.astype(F32) * scale for z in (x, y)]
        for e in (0, 1):
            rows = slice(e * SUB, (e + 1) * SUB)
            both = jnp.concatenate([z[rows] for z in ends], axis=0).astype(BF16)
            out[2 * c + e, a * SUB : (a + 2) * SUB, m * span : (m + 1) * span] = both

    if width == span:
        regroup(2 * spans, per, share, load, store, hold, (4, 2, 1))
    else:
        for g in range(2 * spans):
            xs = gather_lanes([load(g, a) for a in range(per)], share)
            for a in range(0, qlen // SUB, 2):
                store(g, a, a + 1, xs[a], xs[a + 1])


VM = pl.BlockSpec(memory_space=pltpu.VMEM)
FAR = pl.BlockSpec(memory_space=pltpu.HBM)


def call(kernel, ins, outs, scratch=(), name=None, flops=0, out_specs=None, in_specs=None):
    nbytes = sum(math.prod(x.shape) * 2 for x in [*ins, *outs])
    held = nbytes + sum(math.prod(x.shape) * 2 for x in scratch if x.dtype == BF16)
    held += sum(math.prod(x.shape) * 4 for x in scratch if x.dtype == F32)
    return pl.pallas_call(
        kernel,
        out_shape=outs if len(outs) > 1 else outs[0],
        in_specs=in_specs or [VM] * len(ins),
        out_specs=out_specs or ([VM] * len(outs) if len(outs) > 1 else VM),
        scratch_shapes=list(scratch),
        compiler_params=pltpu.CompilerParams(vmem_limit_bytes=held + SPARE),
        cost_estimate=pl.CostEstimate(flops=flops, bytes_accessed=nbytes, transcendentals=0),
        name=name,
    )(*ins)


def shaped(shape, dtype=BF16):
    return jax.ShapeDtypeStruct(shape, dtype)


def local(out_gate, key_gate, value_input, filter_taps, cotangent, block_live):
    ctx = lax.axis_size("ctx")
    dp = lax.axis_size("dp")
    team = TEAM
    tok, chans = key_gate.shape[1:]
    blocks = block_live.shape[1]
    qlen = tok // blocks
    prow = blocks * ctx
    qblocks = qlen // SUB
    share = chans // (ctx * team)
    width = 2 * team * share
    peers = team * ctx
    grid = (blocks, qlen, chans)
    halves = (2 * blocks * chans // min(chans, 128) * 2, qlen // 2, min(chans, 128))
    first, mid, back, last = transform_tables(prow, qlen)
    first, last = jnp.asarray(first), jnp.asarray(last)
    turns = jnp.asarray(np.concatenate([mid, back]))
    spread = jnp.asarray(spread_table(qblocks, 2 * team, share))
    teams = None
    if dp > team:
        teams = [
            [(start + b) * ctx + i for b in range(team) for i in range(ctx)]
            for start in range(0, dp, team)
        ]

    def trade(x, bit):
        return lax.ppermute(x, "dp", [(i, i ^ bit) for i in range(dp)])

    def exchange(x):
        return lax.all_to_all(
            x, ("dp", "ctx"), split_axis=0, concat_axis=0, tiled=True, axis_index_groups=teams
        )

    packed, key, value, cot = call(
        functools.partial(prep_kernel, team),
        [
            pltpu.with_memory_space_constraint(x, pltpu.HBM)
            for x in (
                block_live,
                out_gate.reshape(grid),
                key_gate.reshape(grid),
                value_input.reshape(grid),
                cotangent.reshape(grid),
                filter_taps.reshape(grid),
            )
        ],
        [shaped((peers, qlen + SUB, width))] + [shaped(grid)] * 3,
        scratch=[
            *[pltpu.VMEM(grid, BF16)] * 3,
            pltpu.VMEM((qlen, chans), BF16),
            pltpu.SMEM(block_live.shape, jnp.int32),
            pltpu.VMEM(halves, BF16),
            pltpu.VMEM((peers, SUB, width), F32),
            pltpu.SemaphoreType.DMA((10,)),
        ],
        in_specs=[FAR] * 6,
        name="gate_and_pack",
        flops=10**10,
    )
    tables = [first, spread, turns, last]
    outs = call(
        main_kernel,
        [
            exchange(packed),
            *tables,
        ],
        [shaped((peers, qlen + 2 * SUB, width))],
        scratch=[
            pltpu.VMEM((qblocks, prow * SUB, 2 * width), BF16),
            pltpu.VMEM((prow * SUB, width), BF16),
            pltpu.VMEM((2 * prow, qlen, 2 * width), BF16),
            pltpu.VMEM((qblocks, 2 * prow * SUB, 2 * width), BF16),
            pltpu.VMEM((ctx * blocks, qlen, width), BF16),
            pltpu.VMEM((qblocks // 2 * blocks, ctx * 2 * SUB, width), BF16),
            pltpu.VMEM((qblocks // 2 * blocks, ctx * 2 * SUB, width), BF16),
            pltpu.VMEM((qblocks, prow * SUB, width), F32),
        ],
        name="convolve",
    )
    bit = team
    while bit < dp:
        part = outs[:, qlen:, :]
        total = part.astype(F32) + trade(part, bit).astype(F32)
        outs = lax.dynamic_update_slice(outs, total.astype(BF16), (0, qlen, 0))
        bit *= 2
    recv = exchange(outs)
    mine = recv[:, qlen:, :]
    theirs = trade(mine, 1)
    grads = call(
        post_kernel,
        [recv, key, value, cot],
        [shaped(grid)] * 3,
        scratch=[pltpu.VMEM(grid, BF16)] * 3
        + [pltpu.VMEM(halves, BF16), pltpu.SemaphoreType.DMA((6,))],
        out_specs=[FAR] * 3,
        name="ungate",
    )
    scale = 1.0 / math.sqrt(dp * tok * ctx)
    grad_taps = call(
        functools.partial(finish_kernel, scale),
        [mine, theirs],
        [shaped(grid)],
        scratch=[pltpu.VMEM((2 * peers, 2 * SUB, width), BF16)],
        name="scale_taps",
    )
    return (*[x.reshape(key_gate.shape) for x in grads], grad_taps.reshape(filter_taps.shape))


def solution(mesh):
    return jax.shard_map(
        local,
        mesh=mesh,
        in_specs=(
            P("dp", "ctx", None),
            P("dp", "ctx", None),
            P("dp", "ctx", None),
            P("ctx", None),
            P("dp", "ctx", None),
            P("dp", "ctx"),
        ),
        out_specs=(
            P("dp", "ctx", None),
            P("dp", "ctx", None),
            P("dp", "ctx", None),
            P("ctx", None),
        ),
        check_vma=False,
    )
```

time: 60.6 us -> 55.7 us (0.919)
  starting transfers between devices: 2.28 us -> 0.07 us
  Pallas kernels: 10.4 us -> 8.57 us
  waiting for transfers between devices: 1.81 us -> 0.01 us
  blocking collectives: 45.1 us -> 46.1 us
    ppermute x4 -> x1, starting transfers between devices: 2.28 us -> 0.07 us  [trade(): return lax.ppermute(x, 'dp', [(i, i ^ bit) for i in range(dp)])]
    ppermute x4 -> x1, waiting for transfers between devices: 1.81 us -> 0.01 us  [trade(): return lax.ppermute(x, 'dp', [(i, i ^ bit) for i in range(dp)])]
    pallas_call x6 -> x4, Pallas kernels: 10.4 us -> 8.57 us  [call(): pl.pallas_call(kernel, out_shape=outs if len(outs) > 1 else outs[0], in_s...]
    all_to_all x2, blocking collectives: 45.1 us -> 46.1 us  [exchange(): lax.all_to_all(x, ('dp', 'ctx'), split_axis=0, concat_axis=0, tiled=True,...]
  transfers between devices with their start and end apart: 4 -> 1, of which waited for: 3 -> 0; matrix products, arithmetic and copies ran while one was open for 0% -> 0% of each run, Pallas kernels for 7% -> 3%
where the time goes in v3:
time: 55.7 us; the launch traced here: 55.5 us
  blocking collectives  46.1 us (83%)
  Pallas kernels  8.57 us (15%)
  between operations  0.72 us (1%)
    all_to_all x2, blocking collectives, exchange(): lax.all_to_all(x, ('dp', 'ctx'), split_axis=0, concat_axis=0, tiled=True,...  46.1 us
    pallas_call x4, Pallas kernels, call(): pl.pallas_call(kernel, out_shape=outs if len(outs) > 1 else outs[0], in_s...  8.57 us
  transfers between devices with their start and end apart: 1, of which 0 were waited for; matrix products, arithmetic and copies ran while one was open for 0% of the time, Pallas kernels for 3%

profile of v3, /device:TPU:0, one launch (start us, length us, event | category | flops | bytes accessed | tf_op | source)
XLA Modules:
  0.0 55.5 jit_solution(17590865618047703696)
XLA Ops:
  0.6 0.0 copy-start
  0.6 0.0 copy-start.1
  0.7 0.0 copy-start.2
  0.7 0.0 copy-start.3
  0.7 2.2 %gate_and_pack.1 = (bf16[32,72,128]{2,1,0:T(8,128)(2,1)S(1)}, bf16[4,64,512]{2,1,0:T(8,128)(2,1)S(1)}, bf16[4,64,512]{2,1,0:T(8,128)(2,1)S(1)}, bf16[4,64,512]{2,1,0:T(8,128)(2,1)S(1)}) custom-call(s32[1,4]{1,0:T(1,128)} %live_far.1, bf16[4,64,512]{2,1,0:T(8,128)(2,1)} %bitcast.10, bf16[4,64,512]{2,1,0:T(8,128)(2,1)} %bitcast.11, ...), custom_call_target="tpu_custom_call" | custom-call | flops 10000000000 | bytes 2686984 | tf_op jit(solution)/shard_map/gate_and_pack/pallas_call | solution.py:377
  2.9 24.9 %all_to_all.10.recv = bf16[32,72,128]{2,1,0:T(8,128)(2,1)S(1)} all-to-all(bf16[32,72,128]{2,1,0:T(8,128)(2,1)S(1)} %get-tuple-element.11), channel_id=1, replica_groups=mesh['dp'=4,'ctx'=8] {'dp','ctx'}, dimensions={0} | all-to-all | bytes 1179648 | tf_op jit(solution)/shard_map/all_to_all | solution.py:422
  27.8 0.0 copy-done
  27.8 0.0 copy-done.1
  27.8 0.0 copy-done.2
  27.8 0.0 copy-done.3
  27.8 3.9 %convolve.1 = bf16[32,80,128]{2,1,0:T(8,128)(2,1)S(1)} custom-call(bf16[32,72,128]{2,1,0:T(8,128)(2,1)S(1)} %all_to_all.10.recv, bf16[512,256]{1,0:T(8,128)(2,1)S(1)} %copy-done.3, bf16[128,1024]{1,0:T(8,128)(2,1)S(1)} %copy-done.1, bf16[64,128,128]{2,1,0:T(8,128)(2,1)S(1)} %copy-done, bf16[256,512]{1,0:T(8,128)(2,1)S(1)} %copy-done.2), custom_call_target="tpu_custom_call" | custom-call | bytes 4128768 | tf_op jit(solution)/shard_map/convolve/pallas_call | solution.py:377
  31.6 21.2 %all_to_all.11.recv = bf16[32,80,128]{2,1,0:T(8,128)(2,1)S(1)} all-to-all(bf16[32,80,128]{2,1,0:T(8,128)(2,1)S(1)} %convolve.1), channel_id=1, replica_groups=mesh['dp'=4,'ctx'=8] {'dp','ctx'}, dimensions={0} | all-to-all | bytes 1310720 | tf_op jit(solution)/shard_map/all_to_all | solution.py:422
  52.9 0.1 collective-permute-start
  53.0 1.4 %ungate.1 = (bf16[4,64,512]{2,1,0:T(8,128)(2,1)}, bf16[4,64,512]{2,1,0:T(8,128)(2,1)}, bf16[4,64,512]{2,1,0:T(8,128)(2,1)}) custom-call(bf16[32,80,128]{2,1,0:T(8,128)(2,1)S(1)} %all_to_all.11.recv, bf16[4,64,512]{2,1,0:T(8,128)(2,1)S(1)} %get-tuple-element.12.key, bf16[4,64,512]{2,1,0:T(8,128)(2,1)S(1)} %get-tuple-element.13.value, ...), custom_call_target="tpu_custom_call" | custom-call | bytes 2228224 | tf_op jit(solution)/shard_map/ungate/pallas_call | solution.py:377
  54.4 0.0 collective-permute-done.theirs
  54.4 1.1 %scale_taps.1 = bf16[4,64,512]{2,1,0:T(8,128)(2,1)} custom-call(bf16[32,16,128]{2,1,0:T(8,128)(2,1)S(1)} %slice.4.mine, bf16[32,16,128]{2,1,0:T(8,128)(2,1)S(1)} %collective-permute-done.theirs), custom_call_target="tpu_custom_call" | custom-call | bytes 524288 | tf_op jit(solution)/shard_map/scale_taps/pallas_call | solution.py:377
  (1 shorter events, 0.0 us)
Async XLA Ops:
  0.6 27.1 %copy-start = (bf16[64,128,128]{2,1,0:T(8,128)(2,1)S(1)}, bf16[64,128,128]{2,1,0:T(8,128)(2,1)}, u32[]{:S(2)}) copy-start(bf16[64,128,128]{2,1,0:T(8,128)(2,1)} %constant.10.clone.turns) | copy-start | bytes 6291460
  0.6 27.1 %copy-start.1 = (bf16[128,1024]{1,0:T(8,128)(2,1)S(1)}, bf16[128,1024]{1,0:T(8,128)(2,1)}, u32[]{:S(2)}) copy-start(bf16[128,1024]{1,0:T(8,128)(2,1)} %constant.11.clone.spread) | copy-start | bytes 786436
  0.7 27.1 %copy-start.2 = (bf16[256,512]{1,0:T(8,128)(2,1)S(1)}, bf16[256,512]{1,0:T(8,128)(2,1)}, u32[]{:S(2)}) copy-start(bf16[256,512]{1,0:T(8,128)(2,1)} %constant.9.clone.last) | copy-start | bytes 786436
  0.7 27.1 %copy-start.3 = (bf16[512,256]{1,0:T(8,128)(2,1)S(1)}, bf16[512,256]{1,0:T(8,128)(2,1)}, u32[]{:S(2)}) copy-start(bf16[512,256]{1,0:T(8,128)(2,1)} %constant.8.clone.first) | copy-start | bytes 786436
  52.9 1.5 %collective-permute-start = (bf16[32,16,128]{2,1,0:T(8,128)(2,1)S(1)}, bf16[32,16,128]{2,1,0:T(8,128)(2,1)S(1)}, u32[]{:S(2)}, u32[]{:S(2)}) collective-permute-start(bf16[32,16,128]{2,1,0:T(8,128)(2,1)S(1)} %slice.4.mine), channel_id=1, source_target_pairs={{0,8},{8,0},{16,24},{24,16},{1,9},{9,1},{17,25},{25,17},{2,10},{10... | collective-permute-start | bytes 393224 | tf_op jit(solution)/shard_map/ppermute | solution.py:419

commit v4 on v3

--- a/solution.py
+++ b/solution.py
@@ -1,5 +1,7 @@
 import functools
+import itertools
 import math
+import random
 
 import jax
 import jax.numpy as jnp
@@ -13,7 +15,7 @@
 
 SUB = 8
 TEAM = 4
-PIECES = 4
+SEED = 38
 SPARE = 4 * 1024 * 1024
 F32 = jnp.float32
 BF16 = jnp.bfloat16
@@ -65,7 +67,7 @@
 
 def regroup(groups, count, unit, load, store, hold, steps):
     for place, step in enumerate(steps):
-        for g in range(groups):
+        for g in groups:
             for a in range(count):
                 if a & step:
                     continue
@@ -114,20 +116,14 @@
                 [(key_far, key), (value_far, value), (cot_far, cot), (out_gate_far, out_gate)]
             )
         ])
+    taps_copy.start()
     live_copy.start()
-    for copy in copies[0]:
-        copy.start()
-    taps_copy.start()
-    for group in copies[1:]:
+    for group in copies:
         for copy in group:
             copy.start()
-    live_copy.wait()
 
     def load(g, a):
         part, m = g // spans, g % spans
-        if a == 0 and m == 0:
-            for copy in copies[part]:
-                copy.wait()
         p = a % blocks
         rows = slice(part * size, (part + 1) * size)
         cols = slice(m * span, (m + 1) * span)
@@ -155,11 +151,17 @@
         out[g * per + b, qlen:, :] = y.astype(BF16)
 
     if lanes == span:
-        regroup(parts * spans, 2 * blocks, share, load, store, hold, (1, 2, 4))
         taps_copy.wait()
-        regroup(spans, qlen // SUB, share, load_taps, store_taps, hold_taps, (1, 2, 4))
+        regroup(range(spans), qlen // SUB, share, load_taps, store_taps, hold_taps, (1, 2, 4))
+        live_copy.wait()
+        for part in range(parts):
+            for copy in copies[part]:
+                copy.wait()
+            here = range(part * spans, (part + 1) * spans)
+            regroup(here, 2 * blocks, share, load, store, hold, (1, 2, 4))
     else:
-        taps_copy.wait()
+        for copy in [taps_copy, live_copy, *itertools.chain(*copies)]:
+            copy.wait()
         for g in range(parts * spans):
             xs = gather_lanes([load(g, a) for a in range(2 * blocks)], share)
             for k in range(0, per, 2):
@@ -177,7 +179,7 @@
 
 
 def main_kernel(
-    recv, first, spread, turns, last,
+    seats, recv, first, spread, turns, last,
     out, signal_held, taps_held, rows_held, held, hold, pre, post, taps_out,
 ):
     full_rows, width = recv.shape[1:]
@@ -193,17 +195,17 @@
     for i in range(groups):
         for p in range(0, blocks, 2):
             rows = slice(i * each + p * SUB, i * each + (p + 2) * SUB)
-            ends = [recv[(p + e) * groups + i, qlen:, :].astype(F32) for e in (0, 1)]
+            ends = [recv[seats[p + e][i], qlen:, :].astype(F32) for e in (0, 1)]
             taps_held[rows, :] = jnp.concatenate(ends, axis=0).astype(BF16)
 
     def load(i, b):
-        return recv[b * groups + i, :qlen, :]
+        return recv[seats[b][i], :qlen, :]
 
     def store(i, a, b, x, y):
         rows = slice(i * each + a * SUB, i * each + (a + 2) * SUB)
         signal_held[:, rows, :width] = pair_tiles(x.astype(F32), y.astype(F32), qblocks)
 
-    regroup(groups, blocks, share, load, store, hold, (2, 1))
+    regroup(range(groups), blocks, share, load, store, hold, (2, 1))
     for qb in range(qblocks):
         table = spread[:, qb * width : (qb + 1) * width]
         signal_held[qb, :, width:] = dot(taps_held[...], table).astype(BF16)
@@ -238,7 +240,7 @@
                 held[qb, pl.ds(start, 2 * SUB), :] = both[r, qb]
         return carry
 
-    lax.fori_loop(0, prow // 2, step, 0, unroll=8)
+    lax.fori_loop(0, prow // 2, step, 0, unroll=16)
 
     for qb in range(0, qblocks, 2):
         ends = []
@@ -255,10 +257,12 @@
 
     def store_out(g, a, b, x, y):
         rows = slice(g * 2 * SUB, (g + 1) * 2 * SUB)
-        out[a * groups : (a + 1) * groups, rows, :] = x.reshape(groups, 2 * SUB, width)
-        out[b * groups : (b + 1) * groups, rows, :] = y.reshape(groups, 2 * SUB, width)
-
-    regroup(qblocks // 2, blocks, share, load_out, store_out, post, (1, 2))
+        for i in range(groups):
+            tile = slice(i * 2 * SUB, (i + 1) * 2 * SUB)
+            out[seats[a][i], rows, :] = x[tile]
+            out[seats[b][i], rows, :] = y[tile]
+
+    regroup(range(qblocks // 2), blocks, share, load_out, store_out, post, (1, 2))
     lane = lanes_of((each, width)) // share
     for i in range(groups):
         rows = slice(i * each, (i + 1) * each)
@@ -277,7 +281,7 @@
             step *= 2
         halves = xs[0].reshape(blocks // 2, 2 * SUB, width).astype(BF16)
         for b in range(team):
-            out[b * groups + i, qlen:, :] = halves[b % 2]
+            out[seats[b][i], qlen:, :] = halves[b % 2]
 
 
 def post_kernel(
@@ -325,7 +329,9 @@
                 copies.append(copy)
 
     if width == span:
-        regroup(parts * spans, per, share, load, store, hold, (1, 2, 4))
+        for part in range(parts):
+            here = range(part * spans, (part + 1) * spans)
+            regroup(here, per, share, load, store, hold, (1, 2, 4))
     else:
         for g in range(parts * spans):
             xs = gather_lanes([load(g, a) for a in range(per)], share)
@@ -358,7 +364,7 @@
             out[2 * c + e, a * SUB : (a + 2) * SUB, m * span : (m + 1) * span] = both
 
     if width == span:
-        regroup(2 * spans, per, share, load, store, hold, (4, 2, 1))
+        regroup(range(2 * spans), per, share, load, store, hold, (4, 2, 1))
     else:
         for g in range(2 * spans):
             xs = gather_lanes([load(g, a) for a in range(per)], share)
@@ -408,12 +414,10 @@
     first, last = jnp.asarray(first), jnp.asarray(last)
     turns = jnp.asarray(np.concatenate([mid, back]))
     spread = jnp.asarray(spread_table(qblocks, 2 * team, share))
-    teams = None
-    if dp > team:
-        teams = [
-            [(start + b) * ctx + i for b in range(team) for i in range(ctx)]
-            for start in range(0, dp, team)
-        ]
+    order = np.arange(peers)
+    random.Random(SEED).shuffle(order)
+    seats = np.argsort(order).reshape(team, ctx).tolist()
+    teams = [(start * ctx + order).tolist() for start in range(0, dp, team)]
 
     def trade(x, bit):
         return lax.ppermute(x, "dp", [(i, i ^ bit) for i in range(dp)])
@@ -451,7 +455,7 @@
     )
     tables = [first, spread, turns, last]
     outs = call(
-        main_kernel,
+        functools.partial(main_kernel, seats),
         [
             exchange(packed),
             *tables,

time: 55.7 us -> 53.4 us (0.959)
  blocking collectives: 46.1 us -> 44.4 us
  Pallas kernels: 8.57 us -> 7.96 us
    all_to_all x2, blocking collectives: 46.1 us -> 44.4 us  [exchange(): lax.all_to_all(x, ('dp', 'ctx'), split_axis=0, concat_axis=0, tiled=True,...]
    pallas_call x4, Pallas kernels: 8.57 us -> 7.96 us  [call(): pl.pallas_call(kernel, out_shape=outs if len(outs) > 1 else outs[0], in_s...]
where the time goes in v4:
time: 53.4 us; the launch traced here: 53.1 us
  blocking collectives  44.4 us (83%)
  Pallas kernels  7.96 us (15%)
  between operations  0.72 us (1%)
    all_to_all x2, blocking collectives, exchange(): lax.all_to_all(x, ('dp', 'ctx'), split_axis=0, concat_axis=0, tiled=True,...  44.4 us
    pallas_call x4, Pallas kernels, call(): pl.pallas_call(kernel, out_shape=outs if len(outs) > 1 else outs[0], in_s...  7.96 us
  transfers between devices with their start and end apart: 1, of which 0 were waited for; matrix products, arithmetic and copies ran while one was open for 0% of the time, Pallas kernels for 3%

profile of v4, /device:TPU:0, one launch (start us, length us, event | category | flops | bytes accessed | tf_op | source)
XLA Modules:
  0.0 53.1 jit_solution(4376705014077042980)
XLA Ops:
  0.6 0.0 copy-start
  0.6 0.0 copy-start.1
  0.7 0.0 copy-start.2
  0.7 0.0 copy-start.3
  0.7 2.1 %gate_and_pack.1 = (bf16[32,72,128]{2,1,0:T(8,128)(2,1)S(1)}, bf16[4,64,512]{2,1,0:T(8,128)(2,1)S(1)}, bf16[4,64,512]{2,1,0:T(8,128)(2,1)S(1)}, bf16[4,64,512]{2,1,0:T(8,128)(2,1)S(1)}) custom-call(s32[1,4]{1,0:T(1,128)} %live_far.1, bf16[4,64,512]{2,1,0:T(8,128)(2,1)} %bitcast.10, bf16[4,64,512]{2,1,0:T(8,128)(2,1)} %bitcast.11, ...), custom_call_target="tpu_custom_call" | custom-call | flops 10000000000 | bytes 2686984 | tf_op jit(solution)/shard_map/gate_and_pack/pallas_call | solution.py:383
  2.8 23.7 %all_to_all.10.recv = bf16[32,72,128]{2,1,0:T(8,128)(2,1)S(1)} all-to-all(bf16[32,72,128]{2,1,0:T(8,128)(2,1)S(1)} %get-tuple-element.11), channel_id=1, replica_groups={{31,21,30,12,15,0,16,27,6,7,4,28,9,20,17,8,10,29,18,5,19,1,25,14,22,11,..., dimensions={0} | all-to-all | bytes 1179648 | tf_op jit(solution)/shard_map/all_to_all | solution.py:426
  26.5 0.0 copy-done
  26.5 0.0 copy-done.1
  26.5 0.0 copy-done.2
  26.5 0.0 copy-done.3
  26.5 3.3 %convolve.1 = bf16[32,80,128]{2,1,0:T(8,128)(2,1)S(1)} custom-call(bf16[32,72,128]{2,1,0:T(8,128)(2,1)S(1)} %all_to_all.10.recv, bf16[512,256]{1,0:T(8,128)(2,1)S(1)} %copy-done.3, bf16[128,1024]{1,0:T(8,128)(2,1)S(1)} %copy-done.1, bf16[64,128,128]{2,1,0:T(8,128)(2,1)S(1)} %copy-done, bf16[256,512]{1,0:T(8,128)(2,1)S(1)} %copy-done.2), custom_call_target="tpu_custom_call" | custom-call | bytes 4128768 | tf_op jit(solution)/shard_map/convolve/pallas_call | solution.py:383
  29.8 20.7 %all_to_all.11.recv = bf16[32,80,128]{2,1,0:T(8,128)(2,1)S(1)} all-to-all(bf16[32,80,128]{2,1,0:T(8,128)(2,1)S(1)} %convolve.1), channel_id=1, replica_groups={{31,21,30,12,15,0,16,27,6,7,4,28,9,20,17,8,10,29,18,5,19,1,25,14,22,11,..., dimensions={0} | all-to-all | bytes 1310720 | tf_op jit(solution)/shard_map/all_to_all | solution.py:426
  50.5 0.1 collective-permute-start
  50.5 1.5 %ungate.1 = (bf16[4,64,512]{2,1,0:T(8,128)(2,1)}, bf16[4,64,512]{2,1,0:T(8,128)(2,1)}, bf16[4,64,512]{2,1,0:T(8,128)(2,1)}) custom-call(bf16[32,80,128]{2,1,0:T(8,128)(2,1)S(1)} %all_to_all.11.recv, bf16[4,64,512]{2,1,0:T(8,128)(2,1)S(1)} %get-tuple-element.12.key, bf16[4,64,512]{2,1,0:T(8,128)(2,1)S(1)} %get-tuple-element.13.value, ...), custom_call_target="tpu_custom_call" | custom-call | bytes 2228224 | tf_op jit(solution)/shard_map/ungate/pallas_call | solution.py:383
  52.0 0.0 collective-permute-done.theirs
  52.0 1.1 %scale_taps.1 = bf16[4,64,512]{2,1,0:T(8,128)(2,1)} custom-call(bf16[32,16,128]{2,1,0:T(8,128)(2,1)S(1)} %slice.4.mine, bf16[32,16,128]{2,1,0:T(8,128)(2,1)S(1)} %collective-permute-done.theirs), custom_call_target="tpu_custom_call" | custom-call | bytes 524288 | tf_op jit(solution)/shard_map/scale_taps/pallas_call | solution.py:383
  (1 shorter events, 0.0 us)
Async XLA Ops:
  0.6 25.9 %copy-start = (bf16[64,128,128]{2,1,0:T(8,128)(2,1)S(1)}, bf16[64,128,128]{2,1,0:T(8,128)(2,1)}, u32[]{:S(2)}) copy-start(bf16[64,128,128]{2,1,0:T(8,128)(2,1)} %constant.10.clone.turns) | copy-start | bytes 6291460
  0.6 25.9 %copy-start.1 = (bf16[128,1024]{1,0:T(8,128)(2,1)S(1)}, bf16[128,1024]{1,0:T(8,128)(2,1)}, u32[]{:S(2)}) copy-start(bf16[128,1024]{1,0:T(8,128)(2,1)} %constant.11.clone.spread) | copy-start | bytes 786436
  0.7 25.9 %copy-start.2 = (bf16[256,512]{1,0:T(8,128)(2,1)S(1)}, bf16[256,512]{1,0:T(8,128)(2,1)}, u32[]{:S(2)}) copy-start(bf16[256,512]{1,0:T(8,128)(2,1)} %constant.9.clone.last) | copy-start | bytes 786436
  0.7 25.8 %copy-start.3 = (bf16[512,256]{1,0:T(8,128)(2,1)S(1)}, bf16[512,256]{1,0:T(8,128)(2,1)}, u32[]{:S(2)}) copy-start(bf16[512,256]{1,0:T(8,128)(2,1)} %constant.8.clone.first) | copy-start | bytes 786436
  50.5 1.6 %collective-permute-start = (bf16[32,16,128]{2,1,0:T(8,128)(2,1)S(1)}, bf16[32,16,128]{2,1,0:T(8,128)(2,1)S(1)}, u32[]{:S(2)}, u32[]{:S(2)}) collective-permute-start(bf16[32,16,128]{2,1,0:T(8,128)(2,1)S(1)} %slice.4.mine), channel_id=1, source_target_pairs={{0,8},{8,0},{16,24},{24,16},{1,9},{9,1},{17,25},{25,17},{2,10},{10... | collective-permute-start | bytes 393224 | tf_op jit(solution)/shard_map/ppermute | solution.py:423

commit v5 on v4

--- a/solution.py
+++ b/solution.py
@@ -124,18 +124,21 @@
 
     def load(g, a):
         part, m = g // spans, g % spans
+        if lanes == span and a == 0 and m == 0:
+            for copy in copies[part]:
+                copy.wait()
         p = a % blocks
         rows = slice(part * size, (part + 1) * size)
         cols = slice(m * span, (m + 1) * span)
         if a >= blocks:
-            wide = cot[p, rows, cols].astype(F32)
-            return (wide * out_gate[p, rows, cols].astype(F32)).astype(BF16)
-        alive = live[0, p].astype(F32)
-        kept = key[p, rows, cols].astype(F32) * alive
-        wide = value[p, rows, cols].astype(F32)
-        key_out[p, rows, cols] = kept.astype(BF16)
-        value_out[p, rows, cols] = (wide * alive).astype(BF16)
-        return (kept * wide).astype(BF16)
+            return cot[p, rows, cols] * out_gate[p, rows, cols]
+        dead = live[0, p] == 0
+        none = jnp.zeros((size, span), BF16)
+        kept = jnp.where(dead, none, key[p, rows, cols])
+        kept_value = jnp.where(dead, none, value[p, rows, cols])
+        key_out[p, rows, cols] = kept
+        value_out[p, rows, cols] = kept_value
+        return kept * kept_value
 
     def store(g, a, b, x, y):
         part, m = g // spans, g % spans
@@ -154,11 +157,7 @@
         taps_copy.wait()
         regroup(range(spans), qlen // SUB, share, load_taps, store_taps, hold_taps, (1, 2, 4))
         live_copy.wait()
-        for part in range(parts):
-            for copy in copies[part]:
-                copy.wait()
-            here = range(part * spans, (part + 1) * spans)
-            regroup(here, 2 * blocks, share, load, store, hold, (1, 2, 4))
+        regroup(range(parts * spans), 2 * blocks, share, load, store, hold, (1, 2, 4))
     else:
         for copy in [taps_copy, live_copy, *itertools.chain(*copies)]:
             copy.wait()
@@ -305,13 +304,12 @@
         part, m = g // spans, g % spans
         rows = slice(part * size, (part + 1) * size)
         cols = slice(m * span, (m + 1) * span)
-        x = x.astype(F32)
         if a < blocks:
-            gate_out[a, rows, cols] = (cot[a, rows, cols].astype(F32) * x).astype(BF16)
+            gate_out[a, rows, cols] = cot[a, rows, cols] * x
         else:
             p = a - blocks
-            key_out[p, rows, cols] = (x * value[p, rows, cols].astype(F32)).astype(BF16)
-            value_out[p, rows, cols] = (x * key[p, rows, cols].astype(F32)).astype(BF16)
+            key_out[p, rows, cols] = x * value[p, rows, cols]
+            value_out[p, rows, cols] = x * key[p, rows, cols]
 
     def store(g, a, b, x, y):
         store_one(g, a, x)
@@ -329,9 +327,7 @@
                 copies.append(copy)
 
     if width == span:
-        for part in range(parts):
-            here = range(part * spans, (part + 1) * spans)
-            regroup(here, per, share, load, store, hold, (1, 2, 4))
+        regroup(range(parts * spans), per, share, load, store, hold, (1, 2, 4))
     else:
         for g in range(parts * spans):
             xs = gather_lanes([load(g, a) for a in range(per)], share)

time: 53.4 us -> 53.1 us (level)
  no operation moved by 1% of the time
where the time goes in v5:
time: 53.1 us; the launch traced here: 52.9 us
  blocking collectives  44.4 us (84%)
  Pallas kernels  7.71 us (15%)
  between operations  0.72 us (1%)
    all_to_all x2, blocking collectives, exchange(): lax.all_to_all(x, ('dp', 'ctx'), split_axis=0, concat_axis=0, tiled=True,...  44.4 us
    pallas_call x4, Pallas kernels, call(): pl.pallas_call(kernel, out_shape=outs if len(outs) > 1 else outs[0], in_s...  7.71 us
  transfers between devices with their start and end apart: 1, of which 0 were waited for; matrix products, arithmetic and copies ran while one was open for 0% of the time, Pallas kernels for 3%

profile of v5, /device:TPU:0, one launch (start us, length us, event | category | flops | bytes accessed | tf_op | source)
XLA Modules:
  0.0 52.9 jit_solution(7443187486328016678)
XLA Ops:
  0.6 0.0 copy-start
  0.6 0.0 copy-start.1
  0.7 0.0 copy-start.2
  0.7 0.0 copy-start.3
  0.7 2.0 %gate_and_pack.1 = (bf16[32,72,128]{2,1,0:T(8,128)(2,1)S(1)}, bf16[4,64,512]{2,1,0:T(8,128)(2,1)S(1)}, bf16[4,64,512]{2,1,0:T(8,128)(2,1)S(1)}, bf16[4,64,512]{2,1,0:T(8,128)(2,1)S(1)}) custom-call(s32[1,4]{1,0:T(1,128)} %live_far.1, bf16[4,64,512]{2,1,0:T(8,128)(2,1)} %bitcast.10, bf16[4,64,512]{2,1,0:T(8,128)(2,1)} %bitcast.11, ...), custom_call_target="tpu_custom_call" | custom-call | flops 10000000000 | bytes 2686984 | tf_op jit(solution)/shard_map/gate_and_pack/pallas_call | solution.py:379
  2.7 23.7 %all_to_all.10.recv = bf16[32,72,128]{2,1,0:T(8,128)(2,1)S(1)} all-to-all(bf16[32,72,128]{2,1,0:T(8,128)(2,1)S(1)} %get-tuple-element.11), channel_id=1, replica_groups={{31,21,30,12,15,0,16,27,6,7,4,28,9,20,17,8,10,29,18,5,19,1,25,14,22,11,..., dimensions={0} | all-to-all | bytes 1179648 | tf_op jit(solution)/shard_map/all_to_all | solution.py:422
  26.4 0.0 copy-done
  26.4 0.0 copy-done.1
  26.4 0.0 copy-done.2
  26.4 0.0 copy-done.3
  26.4 3.3 %convolve.1 = bf16[32,80,128]{2,1,0:T(8,128)(2,1)S(1)} custom-call(bf16[32,72,128]{2,1,0:T(8,128)(2,1)S(1)} %all_to_all.10.recv, bf16[512,256]{1,0:T(8,128)(2,1)S(1)} %copy-done.3, bf16[128,1024]{1,0:T(8,128)(2,1)S(1)} %copy-done.1, bf16[64,128,128]{2,1,0:T(8,128)(2,1)S(1)} %copy-done, bf16[256,512]{1,0:T(8,128)(2,1)S(1)} %copy-done.2), custom_call_target="tpu_custom_call" | custom-call | bytes 4128768 | tf_op jit(solution)/shard_map/convolve/pallas_call | solution.py:379
  29.7 20.7 %all_to_all.11.recv = bf16[32,80,128]{2,1,0:T(8,128)(2,1)S(1)} all-to-all(bf16[32,80,128]{2,1,0:T(8,128)(2,1)S(1)} %convolve.1), channel_id=1, replica_groups={{31,21,30,12,15,0,16,27,6,7,4,28,9,20,17,8,10,29,18,5,19,1,25,14,22,11,..., dimensions={0} | all-to-all | bytes 1310720 | tf_op jit(solution)/shard_map/all_to_all | solution.py:422
  50.3 0.1 collective-permute-start
  50.4 1.3 %ungate.1 = (bf16[4,64,512]{2,1,0:T(8,128)(2,1)}, bf16[4,64,512]{2,1,0:T(8,128)(2,1)}, bf16[4,64,512]{2,1,0:T(8,128)(2,1)}) custom-call(bf16[32,80,128]{2,1,0:T(8,128)(2,1)S(1)} %all_to_all.11.recv, bf16[4,64,512]{2,1,0:T(8,128)(2,1)S(1)} %get-tuple-element.12.key, bf16[4,64,512]{2,1,0:T(8,128)(2,1)S(1)} %get-tuple-element.13.value, ...), custom_call_target="tpu_custom_call" | custom-call | bytes 2228224 | tf_op jit(solution)/shard_map/ungate/pallas_call | solution.py:379
  51.8 0.0 collective-permute-done.theirs
  51.8 1.1 %scale_taps.1 = bf16[4,64,512]{2,1,0:T(8,128)(2,1)} custom-call(bf16[32,16,128]{2,1,0:T(8,128)(2,1)S(1)} %slice.4.mine, bf16[32,16,128]{2,1,0:T(8,128)(2,1)S(1)} %collective-permute-done.theirs), custom_call_target="tpu_custom_call" | custom-call | bytes 524288 | tf_op jit(solution)/shard_map/scale_taps/pallas_call | solution.py:379
  (1 shorter events, 0.0 us)
Async XLA Ops:
  0.6 25.8 %copy-start = (bf16[64,128,128]{2,1,0:T(8,128)(2,1)S(1)}, bf16[64,128,128]{2,1,0:T(8,128)(2,1)}, u32[]{:S(2)}) copy-start(bf16[64,128,128]{2,1,0:T(8,128)(2,1)} %constant.10.clone.turns) | copy-start | bytes 6291460
  0.6 25.7 %copy-start.1 = (bf16[128,1024]{1,0:T(8,128)(2,1)S(1)}, bf16[128,1024]{1,0:T(8,128)(2,1)}, u32[]{:S(2)}) copy-start(bf16[128,1024]{1,0:T(8,128)(2,1)} %constant.11.clone.spread) | copy-start | bytes 786436
  0.7 25.7 %copy-start.2 = (bf16[256,512]{1,0:T(8,128)(2,1)S(1)}, bf16[256,512]{1,0:T(8,128)(2,1)}, u32[]{:S(2)}) copy-start(bf16[256,512]{1,0:T(8,128)(2,1)} %constant.9.clone.last) | copy-start | bytes 786436
  0.7 25.7 %copy-start.3 = (bf16[512,256]{1,0:T(8,128)(2,1)S(1)}, bf16[512,256]{1,0:T(8,128)(2,1)}, u32[]{:S(2)}) copy-start(bf16[512,256]{1,0:T(8,128)(2,1)} %constant.8.clone.first) | copy-start | bytes 786436
  50.3 1.4 %collective-permute-start = (bf16[32,16,128]{2,1,0:T(8,128)(2,1)S(1)}, bf16[32,16,128]{2,1,0:T(8,128)(2,1)S(1)}, u32[]{:S(2)}, u32[]{:S(2)}) collective-permute-start(bf16[32,16,128]{2,1,0:T(8,128)(2,1)S(1)} %slice.4.mine), channel_id=1, source_target_pairs={{0,8},{8,0},{16,24},{24,16},{1,9},{9,1},{17,25},{25,17},{2,10},{10... | collective-permute-start | bytes 393224 | tf_op jit(solution)/shard_map/ppermute | solution.py:419

commit v6 on v5

--- a/solution.py
+++ b/solution.py
@@ -65,24 +65,26 @@
     return lax.broadcasted_iota(jnp.int32, shape, len(shape) - 1)
 
 
-def regroup(groups, count, unit, load, store, hold, steps):
-    for place, step in enumerate(steps):
+def skew(x, a, unit):
+    return turn(x, unit * a) if a else x
+
+
+def regroup(groups, count, unit, load, store, hold):
+    if load is not None:
         for g in groups:
             for a in range(count):
-                if a & step:
-                    continue
-                pair = [
-                    load(g, k) if place == 0 else hold[g * count + k] for k in (a, a + step)
-                ]
-                lane = lanes_of(pair[0].shape)
-                low = (lane // (unit * step)) % 2 == 0
-                x = jnp.where(low, pair[0], turn(pair[1], unit * step))
-                y = jnp.where(low, turn(pair[0], -unit * step), pair[1])
-                if place == len(steps) - 1:
-                    store(g, a, a + step, x, y)
-                else:
-                    hold[g * count + a] = x
-                    hold[g * count + a + step] = y
+                hold[g * count + a] = skew(load(g, a), a, unit)
+    for g in groups:
+        xs = [hold[g * count + (-k) % count] for k in range(count)]
+        block = lanes_of(xs[0].shape) // unit
+        step = 1
+        while step < count:
+            moved = (block // step) % 2 == 1
+            xs = [jnp.where(moved, xs[b - step], xs[b]) for b in range(count)]
+            step *= 2
+        xs = [skew(x, -b, unit) for b, x in enumerate(xs)]
+        for b in range(0, count, 2):
+            store(g, b, b + 1, xs[b], xs[b + 1])
 
 
 def gather_lanes(xs, unit):
@@ -155,9 +157,9 @@
 
     if lanes == span:
         taps_copy.wait()
-        regroup(range(spans), qlen // SUB, share, load_taps, store_taps, hold_taps, (1, 2, 4))
+        regroup(range(spans), qlen // SUB, share, load_taps, store_taps, hold_taps)
         live_copy.wait()
-        regroup(range(parts * spans), 2 * blocks, share, load, store, hold, (1, 2, 4))
+        regroup(range(parts * spans), 2 * blocks, share, load, store, hold)
     else:
         for copy in [taps_copy, live_copy, *itertools.chain(*copies)]:
             copy.wait()
@@ -179,7 +181,7 @@
 
 def main_kernel(
     seats, recv, first, spread, turns, last,
-    out, signal_held, taps_held, rows_held, held, hold, pre, post, taps_out,
+    out, signal_held, taps_held, rows_held, held, hold, post, taps_out,
 ):
     full_rows, width = recv.shape[1:]
     prow = turns.shape[0] // 2
@@ -204,7 +206,7 @@
         rows = slice(i * each + a * SUB, i * each + (a + 2) * SUB)
         signal_held[:, rows, :width] = pair_tiles(x.astype(F32), y.astype(F32), qblocks)
 
-    regroup(range(groups), blocks, share, load, store, hold, (2, 1))
+    regroup(range(groups), blocks, share, load, store, hold)
     for qb in range(qblocks):
         table = spread[:, qb * width : (qb + 1) * width]
         signal_held[qb, :, width:] = dot(taps_held[...], table).astype(BF16)
@@ -241,18 +243,25 @@
 
     lax.fori_loop(0, prow // 2, step, 0, unroll=16)
 
+    def reduce_pair(x, y, lane, step):
+        low = (lane // step) % 2 == 0
+        if step >= team:
+            return jnp.where(low, x, y)
+        return jnp.where(low, x, y) + turn(jnp.where(low, y, x), step * share)
+
+    whole_lane = lanes_of((prow * SUB, width)) // share
     for qb in range(0, qblocks, 2):
-        ends = []
-        for e in (0, 1):
-            seq = dot(last[...], held[qb + e])
-            ends.append(seq[:, :width].reshape(groups, blocks, SUB, width))
-            taps_out[qb + e] = seq[:, width:]
+        seqs = [dot(last[...], held[qb + e]) for e in (0, 1)]
+        taps_out[qb // 2] = reduce_pair(seqs[0][:, width:], seqs[1][:, width:], whole_lane, 1)
+        ends = [x[:, :width].reshape(groups, blocks, SUB, width) for x in seqs]
+        both = [
+            jnp.concatenate([x[:, p] for x in ends], axis=1)
+            .reshape(groups * 2 * SUB, width)
+            .astype(BF16)
+            for p in range(blocks)
+        ]
         for p in range(blocks):
-            both = jnp.concatenate([x[:, p] for x in ends], axis=1).astype(BF16)
-            pre[qb // 2 * blocks + p] = both.reshape(groups * 2 * SUB, width)
-
-    def load_out(g, a):
-        return pre[g * blocks + a]
+            post[qb // 2 * blocks + p] = skew(both[p], p, share)
 
     def store_out(g, a, b, x, y):
         rows = slice(g * 2 * SUB, (g + 1) * 2 * SUB)
@@ -261,22 +270,14 @@
             out[seats[a][i], rows, :] = x[tile]
             out[seats[b][i], rows, :] = y[tile]
 
-    regroup(range(qblocks // 2), blocks, share, load_out, store_out, post, (1, 2))
+    regroup(range(qblocks // 2), blocks, share, None, store_out, post)
     lane = lanes_of((each, width)) // share
     for i in range(groups):
         rows = slice(i * each, (i + 1) * each)
-        xs = [taps_out[qb, rows, :] for qb in range(qblocks)]
-        step = 1
-        while step < team:
-            low = (lane // step) % 2 == 0
-            xs = [
-                jnp.where(low, x, y) + turn(jnp.where(low, y, x), step * share)
-                for x, y in zip(xs[::2], xs[1::2])
-            ]
-            step *= 2
+        xs = [taps_out[g, rows, :] for g in range(qblocks // 2)]
+        step = 2
         while len(xs) > 1:
-            low = (lane // step) % 2 == 0
-            xs = [jnp.where(low, x, y) for x, y in zip(xs[::2], xs[1::2])]
+            xs = [reduce_pair(x, y, lane, step) for x, y in zip(xs[::2], xs[1::2])]
             step *= 2
         halves = xs[0].reshape(blocks // 2, 2 * SUB, width).astype(BF16)
         for b in range(team):
@@ -327,7 +328,7 @@
                 copies.append(copy)
 
     if width == span:
-        regroup(range(parts * spans), per, share, load, store, hold, (1, 2, 4))
+        regroup(range(parts * spans), per, share, load, store, hold)
     else:
         for g in range(parts * spans):
             xs = gather_lanes([load(g, a) for a in range(per)], share)
@@ -360,7 +361,7 @@
             out[2 * c + e, a * SUB : (a + 2) * SUB, m * span : (m + 1) * span] = both
 
     if width == span:
-        regroup(range(2 * spans), per, share, load, store, hold, (4, 2, 1))
+        regroup(range(2 * spans), per, share, load, store, hold)
     else:
         for g in range(2 * spans):
             xs = gather_lanes([load(g, a) for a in range(per)], share)
@@ -464,8 +465,7 @@
             pltpu.VMEM((qblocks, 2 * prow * SUB, 2 * width), BF16),
             pltpu.VMEM((ctx * blocks, qlen, width), BF16),
             pltpu.VMEM((qblocks // 2 * blocks, ctx * 2 * SUB, width), BF16),
-            pltpu.VMEM((qblocks // 2 * blocks, ctx * 2 * SUB, width), BF16),
-            pltpu.VMEM((qblocks, prow * SUB, width), F32),
+            pltpu.VMEM((qblocks // 2, prow * SUB, width), F32),
         ],
         name="convolve",
     )

time: 53.1 us -> 52.7 us (level)
  transfers between devices with their start and end apart: 1 -> 1, of which waited for: 0 -> 1; matrix products, arithmetic and copies ran while one was open for 0% -> 0% of each run, Pallas kernels for 3% -> 2%
where the time goes in v6:
time: 52.7 us; the launch traced here: 52.5 us
  blocking collectives  44.4 us (84%)
  Pallas kernels  7.27 us (14%)
  between operations  0.71 us (1%)
    all_to_all x2, blocking collectives, exchange(): lax.all_to_all(x, ('dp', 'ctx'), split_axis=0, concat_axis=0, tiled=True,...  44.4 us
    pallas_call x4, Pallas kernels, call(): pl.pallas_call(kernel, out_shape=outs if len(outs) > 1 else outs[0], in_s...  7.27 us
  transfers between devices with their start and end apart: 1, of which 1 were waited for; matrix products, arithmetic and copies ran while one was open for 0% of the time, Pallas kernels for 2%

profile of v6, /device:TPU:0, one launch (start us, length us, event | category | flops | bytes accessed | tf_op | source)
XLA Modules:
  0.0 52.5 jit_solution(4717847055327010554)
XLA Ops:
  0.6 0.0 copy-start
  0.6 0.0 copy-start.1
  0.7 0.0 copy-start.2
  0.7 0.0 copy-start.3
  0.7 1.9 %gate_and_pack.1 = (bf16[32,72,128]{2,1,0:T(8,128)(2,1)S(1)}, bf16[4,64,512]{2,1,0:T(8,128)(2,1)S(1)}, bf16[4,64,512]{2,1,0:T(8,128)(2,1)S(1)}, bf16[4,64,512]{2,1,0:T(8,128)(2,1)S(1)}) custom-call(s32[1,4]{1,0:T(1,128)} %live_far.1, bf16[4,64,512]{2,1,0:T(8,128)(2,1)} %bitcast.10, bf16[4,64,512]{2,1,0:T(8,128)(2,1)} %bitcast.11, ...), custom_call_target="tpu_custom_call" | custom-call | flops 10000000000 | bytes 2686984 | tf_op jit(solution)/shard_map/gate_and_pack/pallas_call | solution.py:380
  2.6 23.7 %all_to_all.10.recv = bf16[32,72,128]{2,1,0:T(8,128)(2,1)S(1)} all-to-all(bf16[32,72,128]{2,1,0:T(8,128)(2,1)S(1)} %get-tuple-element.11), channel_id=1, replica_groups={{31,21,30,12,15,0,16,27,6,7,4,28,9,20,17,8,10,29,18,5,19,1,25,14,22,11,..., dimensions={0} | all-to-all | bytes 1179648 | tf_op jit(solution)/shard_map/all_to_all | solution.py:423
  26.3 0.0 copy-done
  26.3 0.0 copy-done.1
  26.3 0.0 copy-done.2
  26.3 0.0 copy-done.3
  26.3 3.2 %convolve.1 = bf16[32,80,128]{2,1,0:T(8,128)(2,1)S(1)} custom-call(bf16[32,72,128]{2,1,0:T(8,128)(2,1)S(1)} %all_to_all.10.recv, bf16[512,256]{1,0:T(8,128)(2,1)S(1)} %copy-done.3, bf16[128,1024]{1,0:T(8,128)(2,1)S(1)} %copy-done.1, bf16[64,128,128]{2,1,0:T(8,128)(2,1)S(1)} %copy-done, bf16[256,512]{1,0:T(8,128)(2,1)S(1)} %copy-done.2), custom_call_target="tpu_custom_call" | custom-call | bytes 4128768 | tf_op jit(solution)/shard_map/convolve/pallas_call | solution.py:380
  29.5 20.7 %all_to_all.11.recv = bf16[32,80,128]{2,1,0:T(8,128)(2,1)S(1)} all-to-all(bf16[32,80,128]{2,1,0:T(8,128)(2,1)S(1)} %convolve.1), channel_id=1, replica_groups={{31,21,30,12,15,0,16,27,6,7,4,28,9,20,17,8,10,29,18,5,19,1,25,14,22,11,..., dimensions={0} | all-to-all | bytes 1310720 | tf_op jit(solution)/shard_map/all_to_all | solution.py:423
  50.2 0.1 collective-permute-start
  50.2 1.2 %ungate.1 = (bf16[4,64,512]{2,1,0:T(8,128)(2,1)}, bf16[4,64,512]{2,1,0:T(8,128)(2,1)}, bf16[4,64,512]{2,1,0:T(8,128)(2,1)}) custom-call(bf16[32,80,128]{2,1,0:T(8,128)(2,1)S(1)} %all_to_all.11.recv, bf16[4,64,512]{2,1,0:T(8,128)(2,1)S(1)} %get-tuple-element.12.key, bf16[4,64,512]{2,1,0:T(8,128)(2,1)S(1)} %get-tuple-element.13.value, ...), custom_call_target="tpu_custom_call" | custom-call | bytes 2228224 | tf_op jit(solution)/shard_map/ungate/pallas_call | solution.py:380
  51.5 0.1 collective-permute-done.theirs
  51.6 1.0 %scale_taps.1 = bf16[4,64,512]{2,1,0:T(8,128)(2,1)} custom-call(bf16[32,16,128]{2,1,0:T(8,128)(2,1)S(1)} %slice.4.mine, bf16[32,16,128]{2,1,0:T(8,128)(2,1)S(1)} %collective-permute-done.theirs), custom_call_target="tpu_custom_call" | custom-call | bytes 524288 | tf_op jit(solution)/shard_map/scale_taps/pallas_call | solution.py:380
  (1 shorter events, 0.0 us)
Async XLA Ops:
  0.6 25.6 %copy-start = (bf16[64,128,128]{2,1,0:T(8,128)(2,1)S(1)}, bf16[64,128,128]{2,1,0:T(8,128)(2,1)}, u32[]{:S(2)}) copy-start(bf16[64,128,128]{2,1,0:T(8,128)(2,1)} %constant.10.clone.turns) | copy-start | bytes 6291460
  0.6 25.6 %copy-start.1 = (bf16[128,1024]{1,0:T(8,128)(2,1)S(1)}, bf16[128,1024]{1,0:T(8,128)(2,1)}, u32[]{:S(2)}) copy-start(bf16[128,1024]{1,0:T(8,128)(2,1)} %constant.11.clone.spread) | copy-start | bytes 786436
  0.7 25.6 %copy-start.2 = (bf16[256,512]{1,0:T(8,128)(2,1)S(1)}, bf16[256,512]{1,0:T(8,128)(2,1)}, u32[]{:S(2)}) copy-start(bf16[256,512]{1,0:T(8,128)(2,1)} %constant.9.clone.last) | copy-start | bytes 786436
  0.7 25.6 %copy-start.3 = (bf16[512,256]{1,0:T(8,128)(2,1)S(1)}, bf16[512,256]{1,0:T(8,128)(2,1)}, u32[]{:S(2)}) copy-start(bf16[512,256]{1,0:T(8,128)(2,1)} %constant.8.clone.first) | copy-start | bytes 786436
  50.2 1.4 %collective-permute-start = (bf16[32,16,128]{2,1,0:T(8,128)(2,1)S(1)}, bf16[32,16,128]{2,1,0:T(8,128)(2,1)S(1)}, u32[]{:S(2)}, u32[]{:S(2)}) collective-permute-start(bf16[32,16,128]{2,1,0:T(8,128)(2,1)S(1)} %slice.4.mine), channel_id=1, source_target_pairs={{0,8},{8,0},{16,24},{24,16},{1,9},{9,1},{17,25},{25,17},{2,10},{10... | collective-permute-start | bytes 393224 | tf_op jit(solution)/shard_map/ppermute | solution.py:420

commit v7 on v6

--- a/solution.py
+++ b/solution.py
@@ -15,7 +15,7 @@
 
 SUB = 8
 TEAM = 4
-SEED = 38
+SEED = 84
 SPARE = 4 * 1024 * 1024
 F32 = jnp.float32
 BF16 = jnp.bfloat16

time: 52.7 us -> 52.4 us (level)
  blocking collectives: 44.4 us -> 43.8 us
    all_to_all x2, blocking collectives: 44.4 us -> 43.8 us  [exchange(): lax.all_to_all(x, ('dp', 'ctx'), split_axis=0, concat_axis=0, tiled=True,...]
  transfers between devices with their start and end apart: 1 -> 1, of which waited for: 1 -> 0; matrix products, arithmetic and copies ran while one was open for 0% -> 0% of each run, Pallas kernels for 2% -> 2%
where the time goes in v7:
time: 52.4 us; the launch traced here: 52.3 us
  blocking collectives  43.8 us (84%)
  Pallas kernels  7.28 us (14%)
  between operations  0.71 us (1%)
    all_to_all x2, blocking collectives, exchange(): lax.all_to_all(x, ('dp', 'ctx'), split_axis=0, concat_axis=0, tiled=True,...  43.8 us
    pallas_call x4, Pallas kernels, call(): pl.pallas_call(kernel, out_shape=outs if len(outs) > 1 else outs[0], in_s...  7.28 us
  transfers between devices with their start and end apart: 1, of which 0 were waited for; matrix products, arithmetic and copies ran while one was open for 0% of the time, Pallas kernels for 2%

profile of v7, /device:TPU:0, one launch (start us, length us, event | category | flops | bytes accessed | tf_op | source)
XLA Modules:
  0.0 52.3 jit_solution(11995858578312871624)
XLA Ops:
  0.6 0.0 copy-start
  0.6 0.0 copy-start.1
  0.7 0.0 copy-start.2
  0.7 0.0 copy-start.3
  0.7 1.9 %gate_and_pack.1 = (bf16[32,72,128]{2,1,0:T(8,128)(2,1)S(1)}, bf16[4,64,512]{2,1,0:T(8,128)(2,1)S(1)}, bf16[4,64,512]{2,1,0:T(8,128)(2,1)S(1)}, bf16[4,64,512]{2,1,0:T(8,128)(2,1)S(1)}) custom-call(s32[1,4]{1,0:T(1,128)} %live_far.1, bf16[4,64,512]{2,1,0:T(8,128)(2,1)} %bitcast.10, bf16[4,64,512]{2,1,0:T(8,128)(2,1)} %bitcast.11, ...), custom_call_target="tpu_custom_call" | custom-call | flops 10000000000 | bytes 2686984 | tf_op jit(solution)/shard_map/gate_and_pack/pallas_call | solution.py:380
  2.6 22.8 %all_to_all.10.recv = bf16[32,72,128]{2,1,0:T(8,128)(2,1)S(1)} all-to-all(bf16[32,72,128]{2,1,0:T(8,128)(2,1)S(1)} %get-tuple-element.11), channel_id=1, replica_groups={{23,13,20,12,28,25,19,26,7,2,3,9,5,31,22,30,8,4,11,17,27,14,6,10,21,16,..., dimensions={0} | all-to-all | bytes 1179648 | tf_op jit(solution)/shard_map/all_to_all | solution.py:423
  25.4 0.0 copy-done
  25.4 0.0 copy-done.1
  25.4 0.0 copy-done.2
  25.4 0.0 copy-done.3
  25.4 3.2 %convolve.1 = bf16[32,80,128]{2,1,0:T(8,128)(2,1)S(1)} custom-call(bf16[32,72,128]{2,1,0:T(8,128)(2,1)S(1)} %all_to_all.10.recv, bf16[512,256]{1,0:T(8,128)(2,1)S(1)} %copy-done.3, bf16[128,1024]{1,0:T(8,128)(2,1)S(1)} %copy-done.1, bf16[64,128,128]{2,1,0:T(8,128)(2,1)S(1)} %copy-done, bf16[256,512]{1,0:T(8,128)(2,1)S(1)} %copy-done.2), custom_call_target="tpu_custom_call" | custom-call | bytes 4128768 | tf_op jit(solution)/shard_map/convolve/pallas_call | solution.py:380
  28.6 20.9 %all_to_all.11.recv = bf16[32,80,128]{2,1,0:T(8,128)(2,1)S(1)} all-to-all(bf16[32,80,128]{2,1,0:T(8,128)(2,1)S(1)} %convolve.1), channel_id=1, replica_groups={{23,13,20,12,28,25,19,26,7,2,3,9,5,31,22,30,8,4,11,17,27,14,6,10,21,16,..., dimensions={0} | all-to-all | bytes 1310720 | tf_op jit(solution)/shard_map/all_to_all | solution.py:423
  49.6 0.5 collective-permute-start
  50.0 1.2 %ungate.1 = (bf16[4,64,512]{2,1,0:T(8,128)(2,1)}, bf16[4,64,512]{2,1,0:T(8,128)(2,1)}, bf16[4,64,512]{2,1,0:T(8,128)(2,1)}) custom-call(bf16[32,80,128]{2,1,0:T(8,128)(2,1)S(1)} %all_to_all.11.recv, bf16[4,64,512]{2,1,0:T(8,128)(2,1)S(1)} %get-tuple-element.12.key, bf16[4,64,512]{2,1,0:T(8,128)(2,1)S(1)} %get-tuple-element.13.value, ...), custom_call_target="tpu_custom_call" | custom-call | bytes 2228224 | tf_op jit(solution)/shard_map/ungate/pallas_call | solution.py:380
  51.3 0.0 collective-permute-done.theirs
  51.3 1.0 %scale_taps.1 = bf16[4,64,512]{2,1,0:T(8,128)(2,1)} custom-call(bf16[32,16,128]{2,1,0:T(8,128)(2,1)S(1)} %slice.4.mine, bf16[32,16,128]{2,1,0:T(8,128)(2,1)S(1)} %collective-permute-done.theirs), custom_call_target="tpu_custom_call" | custom-call | bytes 524288 | tf_op jit(solution)/shard_map/scale_taps/pallas_call | solution.py:380
  (1 shorter events, 0.0 us)
Async XLA Ops:
  0.6 24.8 %copy-start = (bf16[64,128,128]{2,1,0:T(8,128)(2,1)S(1)}, bf16[64,128,128]{2,1,0:T(8,128)(2,1)}, u32[]{:S(2)}) copy-start(bf16[64,128,128]{2,1,0:T(8,128)(2,1)} %constant.10.clone.turns) | copy-start | bytes 6291460
  0.6 24.8 %copy-start.1 = (bf16[128,1024]{1,0:T(8,128)(2,1)S(1)}, bf16[128,1024]{1,0:T(8,128)(2,1)}, u32[]{:S(2)}) copy-start(bf16[128,1024]{1,0:T(8,128)(2,1)} %constant.11.clone.spread) | copy-start | bytes 786436
  0.7 24.8 %copy-start.2 = (bf16[256,512]{1,0:T(8,128)(2,1)S(1)}, bf16[256,512]{1,0:T(8,128)(2,1)}, u32[]{:S(2)}) copy-start(bf16[256,512]{1,0:T(8,128)(2,1)} %constant.9.clone.last) | copy-start | bytes 786436
  0.7 24.8 %copy-start.3 = (bf16[512,256]{1,0:T(8,128)(2,1)S(1)}, bf16[512,256]{1,0:T(8,128)(2,1)}, u32[]{:S(2)}) copy-start(bf16[512,256]{1,0:T(8,128)(2,1)} %constant.8.clone.first) | copy-start | bytes 786436
  49.6 1.7 %collective-permute-start = (bf16[32,16,128]{2,1,0:T(8,128)(2,1)S(1)}, bf16[32,16,128]{2,1,0:T(8,128)(2,1)S(1)}, u32[]{:S(2)}, u32[]{:S(2)}) collective-permute-start(bf16[32,16,128]{2,1,0:T(8,128)(2,1)S(1)} %slice.4.mine), channel_id=1, source_target_pairs={{0,8},{8,0},{16,24},{24,16},{1,9},{9,1},{17,25},{25,17},{2,10},{10... | collective-permute-start | bytes 393224 | tf_op jit(solution)/shard_map/ppermute | solution.py:420

commit v8 on v7

--- a/solution.py
+++ b/solution.py
@@ -15,7 +15,7 @@
 
 SUB = 8
 TEAM = 4
-SEED = 84
+SEED = 139
 SPARE = 4 * 1024 * 1024
 F32 = jnp.float32
 BF16 = jnp.bfloat16
@@ -284,9 +284,41 @@
             out[seats[b][i], qlen:, :] = halves[b % 2]
 
 
+def restore_taps(load, scale, stage, hold):
+    _, qlen, chans = stage.shape
+    width = hold.shape[2]
+    share = width // (qlen // SUB)
+    span = min(chans, 128)
+    per = span // share
+
+    def load_one(g, a):
+        return load(g * per + a)
+
+    def store(g, a, b, x, y):
+        ends = [z.astype(F32) * scale for z in (x, y)]
+        for e in (0, 1):
+            rows = slice(e * SUB, (e + 1) * SUB)
+            both = jnp.concatenate([z[rows] for z in ends], axis=0).astype(BF16)
+            stage[e, a * SUB : (a + 2) * SUB, g * span : (g + 1) * span] = both
+
+    if width == span:
+        regroup(range(chans // span), per, share, load_one, store, hold)
+    else:
+        for g in range(chans // span):
+            xs = gather_lanes([load_one(g, a) for a in range(per)], share)
+            for a in range(0, qlen // SUB, 2):
+                store(g, a, a + 1, xs[a], xs[a + 1])
+
+
+def core_half(core):
+    return pl.ds(pl.multiple_of(2 * core, 2), 2)
+
+
 def post_kernel(
-    recv, key, value, cot, gate_far, key_far, value_far, gate_out, key_out, value_out, hold, sems
+    scale, recv, key, value, cot, gate_far, key_far, value_far, taps_far,
+    gate_out, key_out, value_out, stage, hold, hold_taps, sems,
 ):
+    core = lax.rem(lax.axis_index("dp"), 2)
     blocks, qlen, chans = key.shape
     width = recv.shape[2]
     share = width // (2 * blocks)
@@ -334,46 +366,27 @@
             xs = gather_lanes([load(g, a) for a in range(per)], share)
             for a in range(0, 2 * blocks, 2):
                 store(g, a, a + 1, xs[a], xs[a + 1])
+    restore_taps(lambda k: recv[k, qlen:, :], scale, stage, hold_taps)
+    copy = pltpu.make_async_copy(stage, taps_far.at[core_half(core)], sems.at[3 * parts])
+    copy.start()
+    copies.append(copy)
     for copy in copies:
         copy.wait()
 
 
-def finish_kernel(scale, mine, theirs, out, hold):
-    blocks, qlen, chans = out.shape
-    width = mine.shape[2]
-    share = width // (qlen // SUB)
-    span = min(chans, 128)
-    per = span // share
-    spans = chans // span
-    flip = lax.rem(lax.axis_index("dp"), 2) == 0
-
-    def load(g, a):
-        c, m = g // spans, g % spans
-        x, y = mine[m * per + a], theirs[m * per + a]
-        return jnp.where(flip == (c == 0), x, y)
-
-    def store(g, a, b, x, y):
-        c, m = g // spans, g % spans
-        ends = [z.astype(F32) * scale for z in (x, y)]
-        for e in (0, 1):
-            rows = slice(e * SUB, (e + 1) * SUB)
-            both = jnp.concatenate([z[rows] for z in ends], axis=0).astype(BF16)
-            out[2 * c + e, a * SUB : (a + 2) * SUB, m * span : (m + 1) * span] = both
-
-    if width == span:
-        regroup(range(2 * spans), per, share, load, store, hold)
-    else:
-        for g in range(2 * spans):
-            xs = gather_lanes([load(g, a) for a in range(per)], share)
-            for a in range(0, qlen // SUB, 2):
-                store(g, a, a + 1, xs[a], xs[a + 1])
+def finish_kernel(scale, theirs, begun, taps_far, stage, hold, sem):
+    other = 1 - lax.rem(lax.axis_index("dp"), 2)
+    restore_taps(lambda k: theirs[k], scale, stage, hold)
+    copy = pltpu.make_async_copy(stage, taps_far.at[core_half(other)], sem.at[0])
+    copy.start()
+    copy.wait()
 
 
 VM = pl.BlockSpec(memory_space=pltpu.VMEM)
 FAR = pl.BlockSpec(memory_space=pltpu.HBM)
 
 
-def call(kernel, ins, outs, scratch=(), name=None, flops=0, out_specs=None, in_specs=None):
+def call(kernel, ins, outs, scratch=(), name=None, flops=0, aliases=None, out_specs=None, in_specs=None):
     nbytes = sum(math.prod(x.shape) * 2 for x in [*ins, *outs])
     held = nbytes + sum(math.prod(x.shape) * 2 for x in scratch if x.dtype == BF16)
     held += sum(math.prod(x.shape) * 4 for x in scratch if x.dtype == F32)
@@ -383,6 +396,7 @@
         in_specs=in_specs or [VM] * len(ins),
         out_specs=out_specs or ([VM] * len(outs) if len(outs) > 1 else VM),
         scratch_shapes=list(scratch),
+        input_output_aliases=aliases or {},
         compiler_params=pltpu.CompilerParams(vmem_limit_bytes=held + SPARE),
         cost_estimate=pl.CostEstimate(flops=flops, bytes_accessed=nbytes, transcendentals=0),
         name=name,
@@ -478,21 +492,34 @@
     recv = exchange(outs)
     mine = recv[:, qlen:, :]
     theirs = trade(mine, 1)
-    grads = call(
-        post_kernel,
+    scale = 1.0 / math.sqrt(dp * tok * ctx)
+    half = (blocks // 2, qlen, chans)
+    *grads, begun = call(
+        functools.partial(post_kernel, scale),
         [recv, key, value, cot],
-        [shaped(grid)] * 3,
-        scratch=[pltpu.VMEM(grid, BF16)] * 3
-        + [pltpu.VMEM(halves, BF16), pltpu.SemaphoreType.DMA((6,))],
-        out_specs=[FAR] * 3,
+        [shaped(grid)] * 4,
+        scratch=[
+            *[pltpu.VMEM(grid, BF16)] * 3,
+            pltpu.VMEM(half, BF16),
+            pltpu.VMEM(halves, BF16),
+            pltpu.VMEM((peers, 2 * SUB, width), BF16),
+            pltpu.SemaphoreType.DMA((7,)),
+        ],
+        out_specs=[FAR] * 4,
         name="ungate",
     )
-    scale = 1.0 / math.sqrt(dp * tok * ctx)
     grad_taps = call(
         functools.partial(finish_kernel, scale),
-        [mine, theirs],
+        [theirs, pltpu.with_memory_space_constraint(begun, pltpu.HBM)],
         [shaped(grid)],
-        scratch=[pltpu.VMEM((2 * peers, 2 * SUB, width), BF16)],
+        scratch=[
+            pltpu.VMEM(half, BF16),
+            pltpu.VMEM((peers, 2 * SUB, width), BF16),
+            pltpu.SemaphoreType.DMA((1,)),
+        ],
+        in_specs=[VM, FAR],
+        out_specs=FAR,
+        aliases={1: 0},
         name="scale_taps",
     )
     return (*[x.reshape(key_gate.shape) for x in grads], grad_taps.reshape(filter_taps.shape))

time: 52.4 us -> 52.2 us (level)
  no operation moved by 1% of the time
where the time goes in v8:
time: 52.2 us; the launch traced here: 51.8 us
  blocking collectives  43.5 us (83%)
  Pallas kernels  7.18 us (14%)
  between operations  0.71 us (1%)
    all_to_all x2, blocking collectives, exchange(): lax.all_to_all(x, ('dp', 'ctx'), split_axis=0, concat_axis=0, tiled=True,...  43.5 us
    pallas_call x4, Pallas kernels, call(): pl.pallas_call(kernel, out_shape=outs if len(outs) > 1 else outs[0], in_s...  7.18 us
  transfers between devices with their start and end apart: 1, of which 0 were waited for; matrix products, arithmetic and copies ran while one was open for 0% of the time, Pallas kernels for 2%

profile of v8, /device:TPU:0, one launch (start us, length us, event | category | flops | bytes accessed | tf_op | source)
XLA Modules:
  0.0 51.8 jit_solution(6790672391350864724)
XLA Ops:
  0.6 0.0 copy-start
  0.6 0.0 copy-start.1
  0.7 0.0 copy-start.2
  0.7 0.0 copy-start.3
  0.7 1.9 %gate_and_pack.1 = (bf16[32,72,128]{2,1,0:T(8,128)(2,1)S(1)}, bf16[4,64,512]{2,1,0:T(8,128)(2,1)S(1)}, bf16[4,64,512]{2,1,0:T(8,128)(2,1)S(1)}, bf16[4,64,512]{2,1,0:T(8,128)(2,1)S(1)}) custom-call(s32[1,4]{1,0:T(1,128)} %live_far.1, bf16[4,64,512]{2,1,0:T(8,128)(2,1)} %bitcast.10, bf16[4,64,512]{2,1,0:T(8,128)(2,1)} %bitcast.11, ...), custom_call_target="tpu_custom_call" | custom-call | flops 10000000000 | bytes 2686984 | tf_op jit(solution)/shard_map/gate_and_pack/pallas_call | solution.py:393
  2.6 22.6 %all_to_all.10.recv = bf16[32,72,128]{2,1,0:T(8,128)(2,1)S(1)} all-to-all(bf16[32,72,128]{2,1,0:T(8,128)(2,1)S(1)} %get-tuple-element.12), channel_id=1, replica_groups={{12,15,14,1,6,25,29,5,2,7,26,20,24,3,13,18,4,11,8,10,16,31,27,23,9,21,2..., dimensions={0} | all-to-all | bytes 1179648 | tf_op jit(solution)/shard_map/all_to_all | solution.py:437
  25.1 0.0 copy-done
  25.1 0.0 copy-done.1
  25.1 0.0 copy-done.2
  25.1 0.0 copy-done.3
  25.1 3.2 %convolve.1 = bf16[32,80,128]{2,1,0:T(8,128)(2,1)S(1)} custom-call(bf16[32,72,128]{2,1,0:T(8,128)(2,1)S(1)} %all_to_all.10.recv, bf16[512,256]{1,0:T(8,128)(2,1)S(1)} %copy-done.2, bf16[128,1024]{1,0:T(8,128)(2,1)S(1)} %copy-done.1, bf16[64,128,128]{2,1,0:T(8,128)(2,1)S(1)} %copy-done, bf16[256,512]{1,0:T(8,128)(2,1)S(1)} %copy-done.3), custom_call_target="tpu_custom_call" | custom-call | bytes 4128768 | tf_op jit(solution)/shard_map/convolve/pallas_call | solution.py:393
  28.3 21.0 %all_to_all.11.recv = bf16[32,80,128]{2,1,0:T(8,128)(2,1)S(1)} all-to-all(bf16[32,80,128]{2,1,0:T(8,128)(2,1)S(1)} %convolve.1), channel_id=1, replica_groups={{12,15,14,1,6,25,29,5,2,7,26,20,24,3,13,18,4,11,8,10,16,31,27,23,9,21,2..., dimensions={0} | all-to-all | bytes 1310720 | tf_op jit(solution)/shard_map/all_to_all | solution.py:437
  49.3 0.4 collective-permute-start
  49.7 1.3 %ungate.1 = (bf16[4,64,512]{2,1,0:T(8,128)(2,1)}, bf16[4,64,512]{2,1,0:T(8,128)(2,1)}, bf16[4,64,512]{2,1,0:T(8,128)(2,1)}, bf16[4,64,512]{2,1,0:T(8,128)(2,1)}) custom-call(bf16[32,80,128]{2,1,0:T(8,128)(2,1)S(1)} %all_to_all.11.recv, bf16[4,64,512]{2,1,0:T(8,128)(2,1)S(1)} %get-tuple-element.13.key, bf16[4,64,512]{2,1,0:T(8,128)(2,1)S(1)} %get-tuple-element.14.value, ...), custom_call_target="tpu_custom_call" | custom-call | bytes 2490368 | tf_op jit(solution)/shard_map/ungate/pallas_call | solution.py:393
  51.0 0.0 collective-permute-done.theirs
  51.0 0.9 %scale_taps.1 = bf16[4,64,512]{2,1,0:T(8,128)(2,1)} custom-call(bf16[32,16,128]{2,1,0:T(8,128)(2,1)S(1)} %collective-permute-done.theirs, bf16[4,64,512]{2,1,0:T(8,128)(2,1)} %get-tuple-element.19.begun), custom_call_target="tpu_custom_call", output_to_operand_aliasing={{}: (1, {})} | custom-call | bytes 655360 | tf_op jit(solution)/shard_map/scale_taps/pallas_call | solution.py:393
  (1 shorter events, 0.0 us)
Async XLA Ops:
  0.6 24.5 %copy-start = (bf16[64,128,128]{2,1,0:T(8,128)(2,1)S(1)}, bf16[64,128,128]{2,1,0:T(8,128)(2,1)}, u32[]{:S(2)}) copy-start(bf16[64,128,128]{2,1,0:T(8,128)(2,1)} %constant.10.clone.turns) | copy-start | bytes 6291460
  0.6 24.5 %copy-start.1 = (bf16[128,1024]{1,0:T(8,128)(2,1)S(1)}, bf16[128,1024]{1,0:T(8,128)(2,1)}, u32[]{:S(2)}) copy-start(bf16[128,1024]{1,0:T(8,128)(2,1)} %constant.11.clone.spread) | copy-start | bytes 786436
  0.7 24.5 %copy-start.2 = (bf16[512,256]{1,0:T(8,128)(2,1)S(1)}, bf16[512,256]{1,0:T(8,128)(2,1)}, u32[]{:S(2)}) copy-start(bf16[512,256]{1,0:T(8,128)(2,1)} %constant.8.clone.first) | copy-start | bytes 786436
  0.7 24.5 %copy-start.3 = (bf16[256,512]{1,0:T(8,128)(2,1)S(1)}, bf16[256,512]{1,0:T(8,128)(2,1)}, u32[]{:S(2)}) copy-start(bf16[256,512]{1,0:T(8,128)(2,1)} %constant.9.clone.last) | copy-start | bytes 786436
  49.3 1.6 %collective-permute-start = (bf16[32,16,128]{2,1,0:T(8,128)(2,1)S(1)}, bf16[32,16,128]{2,1,0:T(8,128)(2,1)S(1)}, u32[]{:S(2)}, u32[]{:S(2)}) collective-permute-start(bf16[32,16,128]{2,1,0:T(8,128)(2,1)S(1)} %slice.4), channel_id=1, source_target_pairs={{0,8},{8,0},{16,24},{24,16},{1,9},{9,1},{17,25},{25,17},{2,10},{10... | collective-permute-start | bytes 393224 | tf_op jit(solution)/shard_map/ppermute | solution.py:434
